TPU v7x, 512 devices: a whole 4x8x8 slice. The times are simulated.
512 devices in a mesh: frame: 16 (over z_hi, x), space: 32 (over z_lo, y, core).
Axes of the slice: x: 4, y: 8, z: 8 (z_hi: 4, z_lo: 2; z = z_hi * 2 + z_lo), core: 2. Of those that a mesh axis runs over, the one named last changes fastest.
Arguments:
- qkv_now: bfloat16 [4096, 16, 384], P('space', 'frame'), as said below
- past_cache: bfloat16 [16, 4096, 16, 256], P('frame', 'space'), may hold values from -6 to 6
- frame_rank: int32 [16], replicated, may hold values from 0 to 15, each once
- frame_depth: int32 [32], replicated, may hold values from 0 to 16, as said below
- tile_lists: int32 [32, 32], replicated, may hold values from 0 to 1, as said below
Outputs:
- attended: bfloat16 [4096, 2048], P('space', 'frame')
Inputs may be any that keep to these rules, and one draw needn't show every extreme that they name: Entries of qkv_now lie within -5 to 5. `frame_depth`: some tile sees every past frame. `tile_lists`: entry [t, u] is 1 exactly where the distance between tiles t and u around the closed loop of 32 tiles is at most a radius of tile t; the diagonal is 1 and some tile sees all tiles.
All inputs are finite; a program needn't handle non-finite values.
Results may differ from a plain program's by a relative error of at most 0.01.
Values may be sent and summed in bfloat16 or wider, within the bound.
No kernel may reach another device: no remote copies, remote signals or barrier semaphores. Data moves between devices by JAX's collectives and lax.ppermute only.
A program may use at most 64 MiB of HBM per device.

v0:
```python
import math

import jax
import jax.numpy as jnp
from jax import lax
from jax.sharding import PartitionSpec as P

NEG = -1e30


def body(qkv_now, past_cache, frame_rank, frame_depth, tile_lists):
    tok_rows = qkv_now.shape[0]
    head_count = qkv_now.shape[1]
    head_size = qkv_now.shape[2] // 3
    tiles = lax.axis_size("space")
    tile_index = lax.axis_index("space")
    score_scale = 1.0 / math.sqrt(head_size)
    total_rows = tok_rows * tiles
    tile_ids = jnp.arange(tiles, dtype=jnp.int32)
    past = lax.all_to_all(past_cache, "frame", split_axis=2, concat_axis=0, tiled=True)
    frame_count = past.shape[0]
    frame_seen = (frame_rank[None, :] >= frame_count - frame_depth[:, None]).astype(jnp.float32)
    my_column = lax.dynamic_index_in_dim(tile_lists, tile_index, 1, False).astype(jnp.float32)
    key_sets = jnp.concatenate(
        [past.reshape(frame_count * tok_rows, head_count, 2 * head_size), qkv_now[..., head_size:]],
        0,
    )
    seen_table = jnp.concatenate([frame_seen * my_column[:, None], my_column[:, None]], 1)
    groups = seen_table.shape[1]
    gathered = lax.all_gather(qkv_now[..., :head_size], "space", axis=0, tiled=True)
    block_rows = min(total_rows, 512)
    block_count = total_rows // block_rows
    blocks = gathered.reshape(block_count, block_rows, head_count, head_size)
    firsts = jnp.arange(block_count, dtype=jnp.int32) * block_rows

    def one_block(inputs):
        queries, first = inputs
        query_tiles = (first + jnp.arange(block_rows, dtype=jnp.int32)) // tok_rows
        onehot = (query_tiles[:, None] == tile_ids[None, :]).astype(jnp.float32)
        seen = jnp.dot(onehot, seen_table, preferred_element_type=jnp.float32)
        visible = jnp.broadcast_to(seen[:, :, None], (block_rows, groups, tok_rows)).reshape(
            block_rows, groups * tok_rows
        )
        scores = (
            jnp.einsum(
                "qhd,khd->hqk",
                queries,
                key_sets[..., :head_size],
                preferred_element_type=jnp.float32,
            )
            * score_scale
        )
        masked = jnp.where(visible[None] > 0, scores, NEG)
        peak = jnp.max(masked, axis=-1)
        weights = jnp.exp(masked - peak[..., None]) * visible[None]
        totals = jnp.sum(weights, axis=-1)
        weighted = jnp.einsum(
            "hqk,khd->qhd",
            weights.astype(jnp.bfloat16),
            key_sets[..., head_size:],
            preferred_element_type=jnp.float32,
        )
        safe = jnp.maximum(totals, 1.0).T
        share = (weighted / safe[..., None]).astype(jnp.bfloat16)
        return (share, peak.T + jnp.log(safe))

    shares, lse = lax.map(one_block, (blocks, firsts))
    shares = shares.reshape(total_rows, head_count, head_size)
    lse = lse.reshape(total_rows, head_count)
    overall = lax.pmax(lse, "space")
    factor = jnp.exp(lse - overall)
    scaled = shares.astype(jnp.float32) * factor[..., None]
    summed, denominator = (
        lax.psum_scatter(scaled, "space", scatter_dimension=0, tiled=True),
        lax.psum_scatter(factor, "space", scatter_dimension=0, tiled=True),
    )
    result = summed / denominator[..., None]
    return result.reshape(tok_rows, head_count * head_size).astype(jnp.bfloat16)


def solution(mesh):
    in_specs = (P("space", "frame", None), P("frame", "space", None, None), P(), P(), P())
    out_specs = P("space", "frame")
    return jax.shard_map(body, mesh=mesh, in_specs=in_specs, out_specs=out_specs, check_vma=False)
```

profile of v0, /device:TPU:6, one launch (start us, length us, event | category | flops | bytes accessed | tf_op | source)
XLA Modules:
  0.0 570.1 jit_solution(6787443126223372966)
XLA Ops:
  9.1 13.3 %all-to-all-start = ((bf16[1,128,16,256]{3,1,0,2:T(8,128)(2,1)}), bf16[1,128,16,256]{3,1,0,2:T(8,128)(2,1)S(1)}, u32[]{:S(2)}, u32[]{:S(2)}) async-start(bf16[1,128,16,256]{3,1,0,2:T(8,128)(2,1)} %copy.18), calls=%async_computation | async-start | bytes 2097152 | tf_op jit(solution)/shard_map/all_to_all | solution.py:20
  24.2 21.4 %all-to-all-done = bf16[1,128,16,256]{3,1,0,2:T(8,128)(2,1)S(1)} async-done(((bf16[1,128,16,256]{3,1,0,2:T(8,128)(2,1)}), bf16[1,128,16,256]{3,1,0,2:T(8,128)(2,1)S(1)}, u32[]{:S(2)}, u32[]{:S(2)}) %all-to-all-start) | async-done | bytes 1048608 | tf_op jit(solution)/shard_map/all_to_all | solution.py:20
  45.6 47.0 %all-gather.2.cloned.1.call-done = bf16[4096,1,128]{2,0,1:T(8,128)(2,1)} async-done(((bf16[128,1,128]{2,0,1:T(8,128)(2,1)}), bf16[4096,1,128]{2,0,1:T(8,128)(2,1)}) %all-gather.2.cloned.1.call-update) | async-done | bytes 1048592 | tf_op jit(solution)/shard_map/all_gather | solution.py:30
  92.6 123.3 %while.15 = (s32[]{:T(128)}, bf16[8,512,1,128]{3,1,2,0:T(8,128)(2,1)S(1)}, f32[8,512,1]{1,2,0:T(1,128)S(1)}, s32[8]{0:T(128)S(1)}, bf16[32,17]{0,1:T(8,128)(2,1)...) while((s32[]{:T(128)}, ...), condition=%wide.region_3.4_spmd.clone, body=%wide.region_0.3_spmd.clone.sunk | while | flops 582279168 | bytes 59408072 | solution.py:67
  94.1 2.6 broadcast_in_dim.44
  96.7 5.8 %copy.24 = f32[512,2176]{1,0:T(8,128)} copy(f32[512,2176]{0,1:T(8,128)} %bitcast.71) | data formatting | bytes 8912896 | tf_op jit(solution)/shard_map/while/body/eval_jaxpr/broadcast_in_dim;while/body/eval_jaxpr/reshape | solution.py:53
  102.5 3.6 fusion.47
  112.1 5.8 %copy.24 = f32[512,2176]{1,0:T(8,128)} copy(f32[512,2176]{0,1:T(8,128)} %bitcast.71) | data formatting | bytes 8912896 | tf_op jit(solution)/shard_map/while/body/eval_jaxpr/broadcast_in_dim;while/body/eval_jaxpr/reshape | solution.py:53
  117.9 3.6 fusion.47
  127.5 5.8 %copy.24 = f32[512,2176]{1,0:T(8,128)} copy(f32[512,2176]{0,1:T(8,128)} %bitcast.71) | data formatting | bytes 8912896 | tf_op jit(solution)/shard_map/while/body/eval_jaxpr/broadcast_in_dim;while/body/eval_jaxpr/reshape | solution.py:53
  133.3 3.6 fusion.47
  142.9 5.8 %copy.24 = f32[512,2176]{1,0:T(8,128)} copy(f32[512,2176]{0,1:T(8,128)} %bitcast.71) | data formatting | bytes 8912896 | tf_op jit(solution)/shard_map/while/body/eval_jaxpr/broadcast_in_dim;while/body/eval_jaxpr/reshape | solution.py:53
  148.7 3.6 fusion.47
  158.4 5.8 %copy.24 = f32[512,2176]{1,0:T(8,128)} copy(f32[512,2176]{0,1:T(8,128)} %bitcast.71) | data formatting | bytes 8912896 | tf_op jit(solution)/shard_map/while/body/eval_jaxpr/broadcast_in_dim;while/body/eval_jaxpr/reshape | solution.py:53
  164.2 3.6 fusion.47
  173.8 5.8 %copy.24 = f32[512,2176]{1,0:T(8,128)} copy(f32[512,2176]{0,1:T(8,128)} %bitcast.71) | data formatting | bytes 8912896 | tf_op jit(solution)/shard_map/while/body/eval_jaxpr/broadcast_in_dim;while/body/eval_jaxpr/reshape | solution.py:53
  179.6 3.6 fusion.47
  189.2 5.8 %copy.24 = f32[512,2176]{1,0:T(8,128)} copy(f32[512,2176]{0,1:T(8,128)} %bitcast.71) | data formatting | bytes 8912896 | tf_op jit(solution)/shard_map/while/body/eval_jaxpr/broadcast_in_dim;while/body/eval_jaxpr/reshape | solution.py:53
  195.0 3.6 fusion.47
  204.6 5.8 %copy.24 = f32[512,2176]{1,0:T(8,128)} copy(f32[512,2176]{0,1:T(8,128)} %bitcast.71) | data formatting | bytes 8912896 | tf_op jit(solution)/shard_map/while/body/eval_jaxpr/broadcast_in_dim;while/body/eval_jaxpr/reshape | solution.py:53
  210.4 3.6 fusion.47
  215.9 106.9 %pmax.7 = f32[4096,1]{0,1:T(1,128)S(1)} all-reduce(f32[4096,1]{0,1:T(1,128)S(1)} %bitcast.77), channel_id=1, replica_groups=mesh['frame'=16,'space'=32] {'space'}, use_global_device_ids=true, to_apply=%region_4.5 | all-reduce | flops 4096 | bytes 32768 | tf_op jit(solution)/shard_map/pmax | solution.py:70
  326.9 115.6 %reduce-scatter.7.cloned.1.call-done = f32[128,1]{1,0:T(8,128)} async-done(((f32[4096,1]{1,0:T(8,128)}), f32[128,1]{1,0:T(8,128)}) %reduce-scatter.7.cloned.1.call-update) | async-done | bytes 528
  443.3 118.7 %reduce-scatter.5.cloned.1.call-done = f32[128,1,128]{2,0,1:T(8,128)} async-done(((f32[4096,1,128]{2,0,1:T(8,128)}), f32[128,1,128]{2,0,1:T(8,128)}) %reduce-scatter.5.cloned.1.call-update) | async-done | bytes 65552 | tf_op jit(solution)/shard_map/reduce_scatter | solution.py:74
  (110 shorter events, 56.2 us)
Async XLA Ops:
  6.5 17.4 %copy-start = (s32[32,32]{1,0:T(8,128)S(1)}, s32[32,32]{1,0:T(8,128)}, u32[]{:S(2)}) copy-start(s32[32,32]{1,0:T(8,128)} %param.11) | copy-start | bytes 12292
  6.5 39.0 %slice-start = ((bf16[128,1,384]{2,0,1:T(8,128)(2,1)}), bf16[128,1,256]{2,0,1:T(8,128)(2,1)S(1)}, s32[]{:S(2)}) async-start(bf16[128,1,384]{2,0,1:T(8,128)(2,1)} %param.7), calls=%async_computation.6 | async-start | bytes 131072 | tf_op jit(solution)/shard_map/slice | solution.py:25
  6.5 17.5 %copy-start.3 = (s32[32]{0:T(128)S(1)}, s32[32]{0:T(128)}, u32[]{:S(2)}) copy-start(s32[32]{0:T(128)} %param.10) | copy-start | bytes 388
  6.5 17.5 %copy-start.2 = (s32[16]{0:T(128)S(1)}, s32[16]{0:T(128)}, u32[]{:S(2)}) copy-start(s32[16]{0:T(128)} %param.9) | copy-start | bytes 196
  9.1 36.5 %all-to-all-start = ((bf16[1,128,16,256]{3,1,0,2:T(8,128)(2,1)}), bf16[1,128,16,256]{3,1,0,2:T(8,128)(2,1)S(1)}, u32[]{:S(2)}, u32[]{:S(2)}) async-start(bf16[1,128,16,256]{3,1,0,2:T(8,128)(2,1)} %copy.18), calls=%async_computation | async-start | bytes 2097152 | tf_op jit(solution)/shard_map/all_to_all | solution.py:20
  22.4 70.2 %all-gather.2.cloned.1.call-start = ((), (), s32[]{:S(2)}) async-start(), calls=%async_computation.3 | async-start | bytes 1081344 | tf_op jit(solution)/shard_map/all_gather | solution.py:30
  23.8 418.6 %reduce-scatter.7.cloned.1.call-start = ((), (), s32[]{:S(2)}) async-start(), calls=%async_computation.5 | async-start | bytes 2162688
  102.5 3.7 copy-start.1
  117.9 3.7 copy-start.1
  133.3 3.7 copy-start.1
  148.7 3.7 copy-start.1
  164.2 3.7 copy-start.1
  179.6 3.7 copy-start.1
  195.0 3.7 copy-start.1
  210.4 3.7 copy-start.1
  324.8 237.2 %reduce-scatter.5.cloned.1.call-start = ((), (), s32[]{:S(2)}) async-start(), calls=%async_computation.4 | async-start | bytes 2162688 | tf_op jit(solution)/shard_map/reduce_scatter | solution.py:74
Sparse Core Ops, SparseCore 0:
  25.3 67.2 all-gather.1
  325.0 117.4 reduce-scatter.6
  445.5 116.4 reduce-scatter.4
where the time goes:
time: 571 us; the launch traced here: 570 us
  waiting for transfers between devices  303 us (53%)
  blocking collectives  107 us (19%)
  local copies, waits for them, and re-layouts  79.4 us (14%)
  matrix products  38.5 us (7%)
  other arithmetic  15.9 us (3%)
  starting transfers between devices  13.4 us (2%)
  between operations  13.2 us (2%)
    reduce_scatter x1, waiting for transfers between devices, body(): lax.psum_scatter(scaled, 'space', scatter_dimension=0, tiled=True)  119 us
    unnamed x4, waiting for transfers between devices  116 us
    pmax x1, blocking collectives, body(): overall = lax.pmax(lse, 'space')  107 us
    all_gather x1, waiting for transfers between devices, body(): lax.all_gather(qkv_now[..., :head_size], 'space', axis=0, tiled=True)  47 us
    reshape x8, local copies, waits for them, and re-layouts, one_block(): masked = jnp.where(visible[None] > 0, scores, NEG)  46.4 us
    dot_general x8, matrix products, one_block(): jnp.einsum('qhd,khd->hqk', queries, key_sets[..., :head_size], preferred_...  28.8 us
    all_to_all x1, waiting for transfers between devices, body(): lax.all_to_all(past_cache, 'frame', split_axis=2, concat_axis=0, tiled=True)  21.4 us
    broadcast_in_dim x8, local copies, waits for them, and re-layouts, one_block(): jnp.broadcast_to(seen[:, :, None], (block_rows, groups, tok_rows))  20.7 us
  transfers between devices with their start and end apart: 4, of which 4 were waited for; matrix products, arithmetic and copies ran while one was open for 1% of the time, Pallas kernels for 0%

commit v1 on v0

v1 whole, which is shorter than its diff:
```python
import functools
import math

import jax
import jax.numpy as jnp
from jax import lax
from jax.experimental import pallas as pl
from jax.experimental.pallas import tpu as pltpu
from jax.sharding import PartitionSpec as P

NEG = -1e30
LSE_ROWS = 16


def slot_buckets(slots):
    sizes = [size for size in (2, 4, 6, 9, 13) if size < slots]
    return sizes + [slots]


def attend_kernel(
    scale, table, q_ref, past_own, now_own, past_other, now_other, out_ref, keys, values, scores, probs, lse_cols
):
    tiles, tok, size = q_ref.shape
    slots = past_own.shape[0] + 1
    width = 2 * tok
    ones = jnp.ones((tok, size), jnp.bfloat16)
    for slot in range(slots):
        for which, (past, now) in enumerate(((past_own, now_own), (past_other, now_other))):
            block = now[...] if slot == 0 else past[table[slot - 1]]
            first = (2 * slot + which) * tok
            keys[first : first + tok, :] = block[:, :size]
            values[first : first + tok, :size] = block[:, size:]
            values[first : first + tok, size:] = ones
    lse_cols[...] = jnp.full(lse_cols.shape, NEG, jnp.float32)
    lanes = lax.broadcasted_iota(jnp.int32, (tok, tok), 1)
    buckets = slot_buckets(slots)

    def one_pair(pair, _):
        base = slots - 1 + pair * 8
        tile_a, tile_b = table[base], table[base + 1]
        place_a, place_b = table[base + 2], table[base + 3]
        limits = ((table[base + 4], table[base + 5]), (table[base + 6], table[base + 7]))
        most = jnp.maximum(
            jnp.maximum(limits[0][0], limits[0][1]), jnp.maximum(limits[1][0], limits[1][1])
        )

        @pl.when(most == 0)
        def _():
            out_ref[tile_a, :tok, :] = jnp.zeros((tok, size), jnp.bfloat16)
            out_ref[tile_b, :tok, :] = jnp.zeros((tok, size), jnp.bfloat16)

        def work(count):
            queries = jnp.concatenate([q_ref[place_a], q_ref[place_b]], 0)
            peak = None
            for slot in range(count):
                cut = slice(slot * width, (slot + 1) * width)
                raw = lax.dot_general(
                    queries, keys[cut, :], (((1,), (1,)), ((), ())), preferred_element_type=jnp.float32
                )
                rows = []
                for half in range(2):
                    row = []
                    for which in range(2):
                        block = raw[half * tok : (half + 1) * tok, which * tok : (which + 1) * tok]
                        shift = jnp.where(slot < limits[half][which], 0.0, NEG)
                        row.append(block + shift)
                    rows.append(row)
                for half in range(2):
                    for which in range(2):
                        scores[
                            half * tok : (half + 1) * tok,
                            slot * width + which * tok : slot * width + (which + 1) * tok,
                        ] = rows[half][which]
                best = jnp.concatenate([jnp.maximum(row[0], row[1]) for row in rows], 0)
                peak = best if peak is None else jnp.maximum(peak, best)
            peak = jnp.max(peak, axis=1, keepdims=True)
            for slot in range(count):
                cut = slice(slot * width, (slot + 1) * width)
                probs[:, cut] = jnp.exp2(
                    (scores[:, cut] - peak) * (scale * math.log2(math.e))
                ).astype(jnp.bfloat16)
            summed = jnp.dot(
                probs[:, : count * width], values[: count * width, :], preferred_element_type=jnp.float32
            )
            total = summed[:, size:]
            share = (summed[:, :size] / total).astype(jnp.bfloat16)
            out_ref[tile_a, :tok, :] = share[:tok]
            out_ref[tile_b, :tok, :] = share[tok:]
            lse = peak * scale + jnp.log(total)
            cols = jnp.where(lanes == tile_a, lse[:tok], lse_cols[...])
            lse_cols[...] = jnp.where(lanes == tile_b, lse[tok:], cols)

        low = 0
        for count in buckets:
            pl.when((most > low) & (most <= count))(functools.partial(work, count))
            low = count
        return 0

    lax.fori_loop(0, tiles // 2, one_pair, 0)
    lse = lse_cols[...].T[:tiles]
    high = lse.astype(jnp.bfloat16).astype(jnp.float32)
    rest = lse - high
    middle = rest.astype(jnp.bfloat16).astype(jnp.float32)
    low_part = rest - middle
    row_ids = lax.broadcasted_iota(jnp.int32, (LSE_ROWS, tok), 0)
    for tile in range(tiles):
        rows = jnp.where(row_ids == 0, high[tile : tile + 1], 0.0)
        rows = jnp.where(row_ids == 1, middle[tile : tile + 1], rows)
        rows = jnp.where(row_ids == 2, low_part[tile : tile + 1], rows)
        out_ref[tile, tok : tok + LSE_ROWS, :] = rows.astype(jnp.bfloat16)


def combine_kernel(in_ref, out_ref):
    tiles = in_ref.shape[0]
    tok, size = out_ref.shape
    lse = jnp.concatenate(
        [
            jnp.sum(in_ref[tile, tok : tok + LSE_ROWS, :].astype(jnp.float32), axis=0, keepdims=True)
            for tile in range(tiles)
        ],
        0,
    )
    factor = jnp.exp(lse - jnp.max(lse, axis=0, keepdims=True))
    factor = factor / jnp.sum(factor, axis=0, keepdims=True)
    if tiles < tok:
        factor = jnp.concatenate([factor, jnp.zeros((tok - tiles, tok), jnp.float32)], 0)
    factor = factor.T
    total = jnp.zeros((tok, size), jnp.float32)
    for tile in range(tiles):
        total += in_ref[tile, :tok, :].astype(jnp.float32) * factor[:, tile : tile + 1]
    out_ref[...] = total.astype(jnp.bfloat16)


def work_table(frame_rank, frame_depth, tile_lists, position, core, tiles, frames):
    ids = jnp.arange(frames, dtype=jnp.int32)
    by_rank = jnp.sum(
        jnp.where(frame_rank[None, :] == (frames - 1 - ids)[:, None], ids[None, :], 0), axis=1
    )
    own = 2 * position + core
    mine = tile_lists.reshape(tiles, 2, 2 * tiles)
    mine = lax.dynamic_index_in_dim(mine, core, 1, False)
    sees_own = lax.dynamic_index_in_dim(mine, own, 1, False)
    sees_other = lax.dynamic_index_in_dim(mine, own + 1 - 2 * core, 1, False)
    depth = lax.dynamic_index_in_dim(frame_depth.reshape(tiles, 2), core, 1, False) + 1
    own_slots = jnp.where(sees_own == 1, depth, 0)
    other_slots = jnp.where(sees_other == 1, depth, 0)
    most = jnp.maximum(own_slots, other_slots)
    tile_ids = jnp.arange(tiles, dtype=jnp.int32)
    before = (most[None, :] > most[:, None]) | (
        (most[None, :] == most[:, None]) & (tile_ids[None, :] < tile_ids[:, None])
    )
    rank = jnp.sum(before.astype(jnp.int32), axis=1)
    chosen = rank[None, :] == tile_ids[:, None]

    def ordered(values):
        return jnp.sum(jnp.where(chosen, values[None, :], 0), axis=1)

    tile = ordered(tile_ids)
    place = ordered(tile_ids ^ position)
    first, second = ordered(own_slots), ordered(other_slots)
    pairs = jnp.stack([tile, place, first, second], 1).reshape(tiles // 2, 2, 4)
    pairs = jnp.concatenate(
        [pairs[:, :, 0], pairs[:, :, 1], pairs[:, 0, 2:], pairs[:, 1, 2:]], axis=1
    ).reshape(-1)
    return jnp.concatenate([by_rank, pairs]).astype(jnp.int32)


def body(qkv_now, past_cache, frame_rank, frame_depth, tile_lists):
    tok = qkv_now.shape[0]
    size = qkv_now.shape[2] // 3
    space = lax.axis_size("space")
    frames = lax.axis_size("frame")
    tiles = space // 2
    index = lax.axis_index("space")
    position, core = index // 2, index % 2
    scale = 1.0 / math.sqrt(size)

    def swap(array, bit):
        return lax.ppermute(array, "space", [(i, i ^ bit) for i in range(space)])

    by_head = past_cache[0].transpose(1, 0, 2)
    past_own = lax.all_to_all(by_head, "frame", split_axis=0, concat_axis=0, tiled=True)

    now = qkv_now[:, 0, :]
    queries = now[None, :, :size]
    bit = 2
    while bit < space:
        queries = jnp.concatenate([queries, swap(queries, bit)], 0)
        bit *= 2
    now_own = now[:, size:]
    now_other = swap(now_own, 1)
    table = work_table(frame_rank, frame_depth, tile_lists, position, core, tiles, frames)

    past_other = swap(past_own, 1)
    slots = frames + 1
    vmem = pl.BlockSpec(memory_space=pltpu.VMEM)
    partial = pl.pallas_call(
        functools.partial(attend_kernel, scale),
        out_shape=jax.ShapeDtypeStruct((tiles, tok + LSE_ROWS, size), jnp.bfloat16),
        in_specs=[pl.BlockSpec(memory_space=pltpu.SMEM)] + [vmem] * 5,
        out_specs=vmem,
        scratch_shapes=[
            pltpu.VMEM((2 * slots * tok, size), jnp.bfloat16),
            pltpu.VMEM((2 * slots * tok, 2 * size), jnp.bfloat16),
            pltpu.VMEM((2 * tok, 2 * slots * tok), jnp.float32),
            pltpu.VMEM((2 * tok, 2 * slots * tok), jnp.bfloat16),
            pltpu.VMEM((tok, tok), jnp.float32),
        ],
        compiler_params=pltpu.CompilerParams(vmem_limit_bytes=40 * 2**20),
        name="attend",
    )(table, queries, past_own, now_own, past_other, now_other)

    groups = [[2 * place + which for place in range(tiles)] for which in range(2)]
    received = lax.all_to_all(
        partial, "space", split_axis=0, concat_axis=0, axis_index_groups=groups, tiled=True
    )
    return pl.pallas_call(
        combine_kernel,
        out_shape=jax.ShapeDtypeStruct((tok, size), jnp.bfloat16),
        in_specs=[vmem],
        out_specs=vmem,
        name="combine",
    )(received)


def solution(mesh):
    in_specs = (P("space", "frame", None), P("frame", "space", None, None), P(), P(), P())
    out_specs = P("space", "frame")
    return jax.shard_map(body, mesh=mesh, in_specs=in_specs, out_specs=out_specs, check_vma=False)
```

time: 571 us -> 115 us (0.20)
  the two profiles are of different devices: /device:TPU:6 before, /device:TPU:8 now
where the time goes in v1:
time: 115 us; the launch traced here: 114 us
  starting transfers between devices  40.9 us (36%)
  waiting for transfers between devices  29.7 us (26%)
  blocking collectives  24.6 us (21%)
  Pallas kernels  13.3 us (12%)
  local copies, waits for them, and re-layouts  4.56 us (4%)
    ppermute x6, starting transfers between devices, swap(): return lax.ppermute(array, 'space', [(i, i ^ bit) for i in range(space)])  27.9 us
    all_to_all x1, blocking collectives, body(): lax.all_to_all(partial, 'space', split_axis=0, concat_axis=0, axis_index_...  24.6 us
    all_to_all x1, waiting for transfers between devices, body(): lax.all_to_all(by_head, 'frame', split_axis=0, concat_axis=0, tiled=True)  16.4 us
    ppermute x6, waiting for transfers between devices, swap(): return lax.ppermute(array, 'space', [(i, i ^ bit) for i in range(space)])  13.3 us
    all_to_all x1, starting transfers between devices, body(): lax.all_to_all(by_head, 'frame', split_axis=0, concat_axis=0, tiled=True)  13 us
    pallas_call x1, Pallas kernels, body(): pl.pallas_call(functools.partial(attend_kernel, scale), out_shape=jax.Sha...  11 us
    unnamed x15, local copies, waits for them, and re-layouts  3.42 us
  transfers between devices with their start and end apart: 7, of which 4 were waited for; matrix products, arithmetic and copies ran while one was open for 2% of the time, Pallas kernels for 0%

profile of v1, /device:TPU:8, one launch (start us, length us, event | category | flops | bytes accessed | tf_op | source)
XLA Modules:
  0.0 114.2 jit_solution(8896466952968784795)
XLA Ops:
  0.0 2.5 %copy.41 = bf16[1,128,16,256]{3,1,2,0:T(8,128)(2,1)} copy(bf16[1,128,16,256]{3,2,1,0:T(8,128)(2,1)} %param.6) | data formatting | bytes 2097152 | tf_op args[1]
  2.6 13.0 %all-to-all-start = ((bf16[16,128,256]{2,1,0:T(8,128)(2,1)}), bf16[16,128,256]{2,1,0:T(8,128)(2,1)S(1)}, u32[]{:S(2)}, u32[]{:S(2)}) async-start(bf16[16,128,256]{2,1,0:T(8,128)(2,1)} %bitcast.24), calls=%async_computation | async-start | bytes 2097152 | tf_op jit(solution)/shard_map/all_to_all | solution.py:182
  15.6 2.4 %collective-permute-start = (bf16[1,128,128]{2,1,0:T(8,128)(2,1)S(1)}, bf16[1,128,128]{2,1,0:T(8,128)(2,1)S(1)}, u32[]{:S(2)}, u32[]{:S(2)}) collective-permute-start(bf16[1,128,128]{2,1,0:T(8,128)(2,1)S(1)} %slice_bitcast_fusion), channel_id=1, source_target_pairs={{0,2},{1,3},{2,0},{3,1},{4,6},{5,7},{6,4},{7,5},{8,10},{9,11},{10,... | collective-permute-start | bytes 98312 | tf_op jit(solution)/shard_map/ppermute | solution.py:179
  18.0 1.9 %collective-permute-start.5 = (bf16[128,256]{1,0:T(8,128)(2,1)S(1)}, bf16[128,256]{1,0:T(8,128)(2,1)S(1)}, u32[]{:S(2)}, u32[]{:S(2)}) collective-permute-start(bf16[128,256]{1,0:T(8,128)(2,1)S(1)} %slice.23.now_own), channel_id=1, source_target_pairs={{0,1},{1,0},{2,3},{3,2},{4,5},{5,4},{6,7},{7,6},{8,9},{9,8},{10,11... | collective-permute-start | bytes 196616 | tf_op jit(solution)/shard_map/ppermute | solution.py:179
  20.0 0.6 copy-done.2
  20.7 0.1 constant_dynamic-slice_fusion.1
  21.0 0.1 copy.31
  21.1 0.1 copy.32
  21.2 0.2 maximum_reduce_fusion
  21.4 0.2 convert_reduce_fusion
  21.6 0.1 select_reduce_fusion.3
  21.8 0.1 copy.34
  22.4 16.4 %all-to-all-done.past_own = bf16[16,128,256]{2,1,0:T(8,128)(2,1)S(1)} async-done(((bf16[16,128,256]{2,1,0:T(8,128)(2,1)}), bf16[16,128,256]{2,1,0:T(8,128)(2,1)S(1)}, u32[]{:S(2)}, u32[]{:S(2)}) %all-to-all-start) | async-done | bytes 1048608 | tf_op jit(solution)/shard_map/all_to_all | solution.py:182
  38.8 1.9 %collective-permute-start.4 = (bf16[16,128,256]{2,1,0:T(8,128)(2,1)S(1)}, bf16[16,128,256]{2,1,0:T(8,128)(2,1)S(1)}, u32[]{:S(2)}, u32[]{:S(2)}) collective-permute-start(bf16[16,128,256]{2,1,0:T(8,128)(2,1)S(1)} %all-to-all-done.past_own), channel_id=1, source_target_pairs={{0,1},{1,0},{2,3},{3,2},{4,5},{5,4},{6,7},{7,6},{8,9},{9,8},{10,11... | collective-permute-start | bytes 3145736 | tf_op jit(solution)/shard_map/ppermute | solution.py:179
  40.7 4.5 %collective-permute-start.1 = (bf16[2,128,128]{2,1,0:T(8,128)(2,1)S(1)}, bf16[2,128,128]{2,1,0:T(8,128)(2,1)S(1)}, u32[]{:S(2)}, u32[]{:S(2)}) collective-permute-start(bf16[2,128,128]{2,1,0:T(8,128)(2,1)S(1)} %pad_maximum_fusion.2), channel_id=1, source_target_pairs={{0,4},{1,5},{2,6},{3,7},{4,0},{5,1},{6,2},{7,3},{8,12},{9,13},{10,... | collective-permute-start | bytes 196616 | tf_op jit(solution)/shard_map/ppermute | solution.py:179
  45.2 0.2 select_reduce_fusion.4
  45.4 3.1 %collective-permute-done.1 = bf16[2,128,128]{2,1,0:T(8,128)(2,1)S(1)} collective-permute-done((bf16[2,128,128]{2,1,0:T(8,128)(2,1)S(1)}, bf16[2,128,128]{2,1,0:T(8,128)(2,1)S(1)}, u32[]{:S(2)}, u32[]{:S(2)}) %collective-permute-start.1) | collective-permute-done | bytes 65568 | tf_op jit(solution)/shard_map/ppermute | solution.py:179
  48.5 6.4 %collective-permute-start.2 = (bf16[4,128,128]{2,1,0:T(8,128)(2,1)S(1)}, bf16[4,128,128]{2,1,0:T(8,128)(2,1)S(1)}, u32[]{:S(2)}, u32[]{:S(2)}) collective-permute-start(bf16[4,128,128]{2,1,0:T(8,128)(2,1)S(1)} %pad_maximum_fusion.1), channel_id=1, source_target_pairs={{0,8},{1,9},{2,10},{3,11},{4,12},{5,13},{6,14},{7,15},{8,0},{9,1},... | collective-permute-start | bytes 393224 | tf_op jit(solution)/shard_map/ppermute | solution.py:179
  55.2 4.7 %collective-permute-done.2 = bf16[4,128,128]{2,1,0:T(8,128)(2,1)S(1)} collective-permute-done((bf16[4,128,128]{2,1,0:T(8,128)(2,1)S(1)}, bf16[4,128,128]{2,1,0:T(8,128)(2,1)S(1)}, u32[]{:S(2)}, u32[]{:S(2)}) %collective-permute-start.2) | collective-permute-done | bytes 131104 | tf_op jit(solution)/shard_map/ppermute | solution.py:179
  59.9 10.8 %collective-permute-start.3 = (bf16[8,128,128]{2,1,0:T(8,128)(2,1)S(1)}, bf16[8,128,128]{2,1,0:T(8,128)(2,1)S(1)}, u32[]{:S(2)}, u32[]{:S(2)}) collective-permute-start(bf16[8,128,128]{2,1,0:T(8,128)(2,1)S(1)} %pad_maximum_fusion), channel_id=1, source_target_pairs={{0,16},{1,17},{2,18},{3,19},{4,20},{5,21},{6,22},{7,23},{8,24},{9,... | collective-permute-start | bytes 786440 | tf_op jit(solution)/shard_map/ppermute | solution.py:179
  70.8 5.5 %collective-permute-done.3 = bf16[8,128,128]{2,1,0:T(8,128)(2,1)S(1)} collective-permute-done((bf16[8,128,128]{2,1,0:T(8,128)(2,1)S(1)}, bf16[8,128,128]{2,1,0:T(8,128)(2,1)S(1)}, u32[]{:S(2)}, u32[]{:S(2)}) %collective-permute-start.3) | collective-permute-done | bytes 262176 | tf_op jit(solution)/shard_map/ppermute | solution.py:179
  76.4 11.0 %attend.1 = bf16[16,144,128]{2,1,0:T(8,128)(2,1)S(1)} custom-call(s32[80]{0:T(128)S(1)} %pad_add_fusion.2.table, bf16[16,128,128]{2,1,0:T(8,128)(2,1)S(1)} %constant_dynamic-update-slice_fusion.q_ref, bf16[16,128,256]{2,1,0:T(8,128)(2,1)S(1)} %all-to-all-done.past_own, bf16[128,256]{1,0:T(8,128)(2,1)S(1)} %slice.23.now_own, ...), custom_call_target="tpu_custom_call" | custom-call | tf_op jit(solution)/shard_map/attend/pallas_call | solution.py:197
  87.4 24.6 %all_to_all.10.in_ref = bf16[16,144,128]{2,1,0:T(8,128)(2,1)} all-to-all(bf16[16,144,128]{2,1,0:T(8,128)(2,1)S(1)} %attend.1), channel_id=1, replica_groups={{0,2,4,6,8,10,12,14,16,18,20,22,24,26,28,30},{1,3,5,7,9,11,13,15,17,19,..., dimensions={0} | all-to-all | bytes 1179648 | tf_op jit(solution)/shard_map/all_to_all | solution.py:214
  112.0 2.2 %combine.1 = bf16[128,128]{1,0:T(8,128)(2,1)} custom-call(bf16[16,144,128]{2,1,0:T(8,128)(2,1)} %all_to_all.10.in_ref), custom_call_target="tpu_custom_call" | custom-call | tf_op jit(solution)/shard_map/combine/pallas_call | solution.py:217
  (38 shorter events, 1.2 us)
Async XLA Ops:
  2.6 13.0 %copy-start = (bf16[128,1,384]{2,0,1:T(8,128)(2,1)S(1)}, bf16[128,1,384]{2,0,1:T(8,128)(2,1)}, u32[]{:S(2)}) copy-start(bf16[128,1,384]{2,0,1:T(8,128)(2,1)} %param.5) | copy-start | bytes 294916
  2.6 36.2 %all-to-all-start = ((bf16[16,128,256]{2,1,0:T(8,128)(2,1)}), bf16[16,128,256]{2,1,0:T(8,128)(2,1)S(1)}, u32[]{:S(2)}, u32[]{:S(2)}) async-start(bf16[16,128,256]{2,1,0:T(8,128)(2,1)} %bitcast.24), calls=%async_computation | async-start | bytes 2097152 | tf_op jit(solution)/shard_map/all_to_all | solution.py:182
  15.6 25.1 %collective-permute-start = (bf16[1,128,128]{2,1,0:T(8,128)(2,1)S(1)}, bf16[1,128,128]{2,1,0:T(8,128)(2,1)S(1)}, u32[]{:S(2)}, u32[]{:S(2)}) collective-permute-start(bf16[1,128,128]{2,1,0:T(8,128)(2,1)S(1)} %slice_bitcast_fusion), channel_id=1, source_target_pairs={{0,2},{1,3},{2,0},{3,1},{4,6},{5,7},{6,4},{7,5},{8,10},{9,11},{10,... | collective-permute-start | bytes 98312 | tf_op jit(solution)/shard_map/ppermute | solution.py:179
  18.0 58.4 %collective-permute-start.5 = (bf16[128,256]{1,0:T(8,128)(2,1)S(1)}, bf16[128,256]{1,0:T(8,128)(2,1)S(1)}, u32[]{:S(2)}, u32[]{:S(2)}) collective-permute-start(bf16[128,256]{1,0:T(8,128)(2,1)S(1)} %slice.23.now_own), channel_id=1, source_target_pairs={{0,1},{1,0},{2,3},{3,2},{4,5},{5,4},{6,7},{7,6},{8,9},{9,8},{10,11... | collective-permute-start | bytes 196616 | tf_op jit(solution)/shard_map/ppermute | solution.py:179
  19.9 0.8 copy-start.1
  19.9 0.7 copy-start.2
  22.4 22.8 %copy-start.3 = (s32[16]{0:T(128)S(1)}, s32[16]{0:T(128)}, u32[]{:S(2)}) copy-start(s32[16]{0:T(128)} %param.7) | copy-start | bytes 196
  38.8 37.6 %collective-permute-start.4 = (bf16[16,128,256]{2,1,0:T(8,128)(2,1)S(1)}, bf16[16,128,256]{2,1,0:T(8,128)(2,1)S(1)}, u32[]{:S(2)}, u32[]{:S(2)}) collective-permute-start(bf16[16,128,256]{2,1,0:T(8,128)(2,1)S(1)} %all-to-all-done.past_own), channel_id=1, source_target_pairs={{0,1},{1,0},{2,3},{3,2},{4,5},{5,4},{6,7},{7,6},{8,9},{9,8},{10,11... | collective-permute-start | bytes 3145736 | tf_op jit(solution)/shard_map/ppermute | solution.py:179
  40.7 7.8 %collective-permute-start.1 = (bf16[2,128,128]{2,1,0:T(8,128)(2,1)S(1)}, bf16[2,128,128]{2,1,0:T(8,128)(2,1)S(1)}, u32[]{:S(2)}, u32[]{:S(2)}) collective-permute-start(bf16[2,128,128]{2,1,0:T(8,128)(2,1)S(1)} %pad_maximum_fusion.2), channel_id=1, source_target_pairs={{0,4},{1,5},{2,6},{3,7},{4,0},{5,1},{6,2},{7,3},{8,12},{9,13},{10,... | collective-permute-start | bytes 196616 | tf_op jit(solution)/shard_map/ppermute | solution.py:179
  48.5 11.3 %collective-permute-start.2 = (bf16[4,128,128]{2,1,0:T(8,128)(2,1)S(1)}, bf16[4,128,128]{2,1,0:T(8,128)(2,1)S(1)}, u32[]{:S(2)}, u32[]{:S(2)}) collective-permute-start(bf16[4,128,128]{2,1,0:T(8,128)(2,1)S(1)} %pad_maximum_fusion.1), channel_id=1, source_target_pairs={{0,8},{1,9},{2,10},{3,11},{4,12},{5,13},{6,14},{7,15},{8,0},{9,1},... | collective-permute-start | bytes 393224 | tf_op jit(solution)/shard_map/ppermute | solution.py:179
  59.9 16.4 %collective-permute-start.3 = (bf16[8,128,128]{2,1,0:T(8,128)(2,1)S(1)}, bf16[8,128,128]{2,1,0:T(8,128)(2,1)S(1)}, u32[]{:S(2)}, u32[]{:S(2)}) collective-permute-start(bf16[8,128,128]{2,1,0:T(8,128)(2,1)S(1)} %pad_maximum_fusion), channel_id=1, source_target_pairs={{0,16},{1,17},{2,18},{3,19},{4,20},{5,21},{6,22},{7,23},{8,24},{9,... | collective-permute-start | bytes 786440 | tf_op jit(solution)/shard_map/ppermute | solution.py:179

commit v2 on v1

v2 whole, which is shorter than its diff:
```python
import functools
import math

import jax
import jax.numpy as jnp
from jax import lax
from jax.experimental import pallas as pl
from jax.experimental.pallas import tpu as pltpu
from jax.sharding import PartitionSpec as P

NEG = -1e30
LSE_ROWS = 16
GROUP = 4


def slot_buckets(slots):
    sizes = [size for size in (1, 2, 3, 4, 5, 6, 7, 8, 9, 11, 13, 15) if size < slots]
    return sizes + [slots]


def attend_kernel(
    scale, table, q_ref, past_own, now_own, past_other, now_other, out_ref, values, scores
):
    tiles, tok, size = q_ref.shape
    slots = past_own.shape[0] + 1
    sources = ((past_own, now_own), (past_other, now_other))

    def block_of(slot, which):
        past, now = sources[which]
        return now[...] if slot == 0 else past[table[slot - 1]]

    def first_of(slot, which):
        return (2 * slot + which) * tok

    for slot in range(slots):
        for which in range(2):
            first = first_of(slot, which)
            values[:size, first : first + tok] = block_of(slot, which)[:, size:].T
    values[size:, :] = jnp.ones((LSE_ROWS, 2 * slots * tok), jnp.bfloat16)
    row_ids = lax.broadcasted_iota(jnp.int32, (LSE_ROWS, tok), 0)
    buckets = slot_buckets(slots)

    def one_group(group, _):
        base = slots - 1 + group * (4 * GROUP)
        group_tiles = [table[base + member * 4] for member in range(GROUP)]
        places = [table[base + member * 4 + 1] for member in range(GROUP)]
        limits = [(table[base + member * 4 + 2], table[base + member * 4 + 3]) for member in range(GROUP)]
        most = functools.reduce(jnp.maximum, [limit for both in limits for limit in both])

        @pl.when(most == 0)
        def _():
            for tile in group_tiles:
                out_ref[tile, :size, :] = jnp.zeros((size, tok), jnp.bfloat16)
                out_ref[tile, size:, :] = jnp.where(row_ids == 0, NEG, 0.0).astype(jnp.bfloat16)

        def work(count):
            queries = jnp.concatenate([q_ref[place].T for place in places], 1)
            peaks = [jnp.full((8, tok), NEG, jnp.float32) for _ in range(GROUP)]
            for slot in range(count):
                for which in range(2):
                    first = first_of(slot, which)
                    raw = jnp.dot(
                        block_of(slot, which)[:, :size], queries, preferred_element_type=jnp.float32
                    )
                    scores[first : first + tok, :] = raw
                    for half in range(GROUP):
                        best = jnp.max(
                            raw[:, half * tok : (half + 1) * tok].reshape(tok // 8, 8, tok), axis=0
                        )
                        best = jnp.where(slot < limits[half][which], best, NEG)
                        peaks[half] = jnp.maximum(peaks[half], best)
            peaks = [jnp.max(peak, axis=0, keepdims=True) for peak in peaks]
            summed = None
            for slot in range(count):
                chunk = []
                for which in range(2):
                    first = first_of(slot, which)
                    shift = jnp.concatenate(
                        [jnp.where(slot < limits[half][which], peaks[half], -NEG) for half in range(GROUP)],
                        1,
                    )
                    chunk.append(
                        jnp.exp2(
                            (scores[first : first + tok, :] - shift) * (scale * math.log2(math.e))
                        ).astype(jnp.bfloat16)
                    )
                start = first_of(slot, 0)
                term = jnp.dot(
                    values[:, start : start + 2 * tok],
                    jnp.concatenate(chunk, 0),
                    preferred_element_type=jnp.float32,
                )
                summed = term if summed is None else summed + term
            total = jnp.maximum(summed[size : size + 1, :], 1.0)
            share = (summed[:size, :] / total).astype(jnp.bfloat16)
            lse = jnp.concatenate(peaks, 1) * scale + jnp.log(total)
            high = lse.astype(jnp.bfloat16).astype(jnp.float32)
            rest = lse - high
            middle = rest.astype(jnp.bfloat16).astype(jnp.float32)
            low_part = rest - middle
            for half, tile in enumerate(group_tiles):
                cut = slice(half * tok, (half + 1) * tok)
                rows = jnp.where(row_ids == 0, high[:, cut], 0.0)
                rows = jnp.where(row_ids == 1, middle[:, cut], rows)
                rows = jnp.where(row_ids == 2, low_part[:, cut], rows)
                out_ref[tile, :size, :] = share[:, cut]
                out_ref[tile, size:, :] = rows.astype(jnp.bfloat16)

        low = 0
        for count in buckets:
            pl.when((most > low) & (most <= count))(functools.partial(work, count))
            low = count
        return 0

    lax.fori_loop(0, tiles // GROUP, one_group, 0)


def attend_call(scale, table, queries, past_own, now_own, past_other, now_other):
    tiles, tok, size = queries.shape
    slots = past_own.shape[0] + 1
    vmem = pl.BlockSpec(memory_space=pltpu.VMEM)
    return pl.pallas_call(
        functools.partial(attend_kernel, scale),
        out_shape=jax.ShapeDtypeStruct((tiles, size + LSE_ROWS, tok), jnp.bfloat16),
        in_specs=[pl.BlockSpec(memory_space=pltpu.SMEM)] + [vmem] * 5,
        out_specs=vmem,
        scratch_shapes=[
            pltpu.VMEM((size + LSE_ROWS, 2 * slots * tok), jnp.bfloat16),
            pltpu.VMEM((2 * slots * tok, GROUP * tok), jnp.float32),
        ],
        compiler_params=pltpu.CompilerParams(vmem_limit_bytes=40 * 2**20),
        name="attend",
    )(table, queries, past_own, now_own, past_other, now_other)


def combine_kernel(in_ref, out_ref):
    tiles = in_ref.shape[0]
    tok, size = out_ref.shape
    lse = jnp.concatenate(
        [
            jnp.sum(in_ref[tile, size:, :].astype(jnp.float32), axis=0, keepdims=True)
            for tile in range(tiles)
        ],
        0,
    )
    factor = jnp.exp(lse - jnp.max(lse, axis=0, keepdims=True))
    factor = factor / jnp.sum(factor, axis=0, keepdims=True)
    total = in_ref[0, :size, :].astype(jnp.float32) * factor[0:1]
    for tile in range(1, tiles):
        total += in_ref[tile, :size, :].astype(jnp.float32) * factor[tile : tile + 1]
    out_ref[...] = total.T.astype(jnp.bfloat16)


def gather_bits(tiles):
    bits = [1 << k for k in range(tiles.bit_length() - 1)]
    return [bits[2], bits[1], bits[0], bits[3]] if len(bits) == 4 else bits[::-1]


def work_table(frame_rank, frame_depth, tile_lists, position, core, tiles, frames):
    ids = jnp.arange(frames, dtype=jnp.int32)
    by_rank = jnp.sum(
        jnp.where(frame_rank[None, :] == (frames - 1 - ids)[:, None], ids[None, :], 0), axis=1
    )
    own = 2 * position + core
    mine = tile_lists.reshape(tiles, 2, 2 * tiles)
    mine = lax.dynamic_index_in_dim(mine, core, 1, False)
    sees_own = lax.dynamic_index_in_dim(mine, own, 1, False)
    sees_other = lax.dynamic_index_in_dim(mine, own + 1 - 2 * core, 1, False)
    depth = lax.dynamic_index_in_dim(frame_depth.reshape(tiles, 2), core, 1, False) + 1
    own_slots = jnp.where(sees_own == 1, depth, 0)
    other_slots = jnp.where(sees_other == 1, depth, 0)
    most = jnp.maximum(own_slots, other_slots)
    tile_ids = jnp.arange(tiles, dtype=jnp.int32)
    before = (most[None, :] > most[:, None]) | (
        (most[None, :] == most[:, None]) & (tile_ids[None, :] < tile_ids[:, None])
    )
    rank = jnp.sum(before.astype(jnp.int32), axis=1)
    chosen = rank[None, :] == tile_ids[:, None]

    def ordered(values):
        return jnp.sum(jnp.where(chosen, values[None, :], 0), axis=1)

    tile = ordered(tile_ids)
    apart = tile_ids ^ position
    place = jnp.zeros_like(tile_ids)
    for k, bit in enumerate(gather_bits(tiles)):
        place = place + jnp.where((apart & bit) != 0, 1 << k, 0)
    place = ordered(place)
    first, second = ordered(own_slots), ordered(other_slots)
    pairs = jnp.stack([tile, place, first, second], 1).reshape(-1)
    return jnp.concatenate([by_rank, pairs]).astype(jnp.int32)


def body(qkv_now, past_cache, frame_rank, frame_depth, tile_lists):
    tok = qkv_now.shape[0]
    size = qkv_now.shape[2] // 3
    space = lax.axis_size("space")
    frames = lax.axis_size("frame")
    tiles = space // 2
    index = lax.axis_index("space")
    position, core = index // 2, index % 2
    scale = 1.0 / math.sqrt(size)

    def swap(array, bit):
        return lax.ppermute(array, "space", [(i, i ^ bit) for i in range(space)])

    by_head = past_cache[0].transpose(1, 0, 2)
    past_own = lax.all_to_all(by_head, "frame", split_axis=0, concat_axis=0, tiled=True)

    now = qkv_now[:, 0, :]
    queries = now[None, :, :size]
    for bit in gather_bits(tiles):
        queries = jnp.concatenate([queries, swap(queries, 2 * bit)], 0)
    now_own = now[:, size:]
    now_other = swap(now_own, 1)
    table = work_table(frame_rank, frame_depth, tile_lists, position, core, tiles, frames)

    past_own, queries = lax.optimization_barrier((past_own, queries))
    past_other = swap(past_own, 1)
    partial = attend_call(scale, table, queries, past_own, now_own, past_other, now_other)
    groups = [[2 * place + which for place in range(tiles)] for which in range(2)]
    received = lax.all_to_all(
        partial, "space", split_axis=0, concat_axis=0, axis_index_groups=groups, tiled=True
    )
    return pl.pallas_call(
        combine_kernel,
        out_shape=jax.ShapeDtypeStruct((tok, size), jnp.bfloat16),
        name="combine",
    )(received)


def solution(mesh):
    in_specs = (P("space", "frame", None), P("frame", "space", None, None), P(), P(), P())
    out_specs = P("space", "frame")
    return jax.shard_map(body, mesh=mesh, in_specs=in_specs, out_specs=out_specs, check_vma=False)
```

time: 115 us -> 88.1 us (0.77)
  the two profiles are of different devices: /device:TPU:8 before, /device:TPU:6 now
where the time goes in v2:
time: 88.1 us; the launch traced here: 87.5 us
  starting transfers between devices  34.9 us (40%)
  blocking collectives  24.5 us (28%)
  waiting for transfers between devices  15.3 us (17%)
  Pallas kernels  7.51 us (9%)
  local copies, waits for them, and re-layouts  4.01 us (5%)
    all_to_all x1, blocking collectives, body(): lax.all_to_all(partial, 'space', split_axis=0, concat_axis=0, axis_index_...  24.5 us
    ppermute x6, starting transfers between devices, swap(): return lax.ppermute(array, 'space', [(i, i ^ bit) for i in range(space)])  21.5 us
    ppermute x6, waiting for transfers between devices, swap(): return lax.ppermute(array, 'space', [(i, i ^ bit) for i in range(space)])  15.3 us
    all_to_all x1, starting transfers between devices, body(): lax.all_to_all(by_head, 'frame', split_axis=0, concat_axis=0, tiled=True)  13.4 us
    pallas_call x1, Pallas kernels, attend_call(): pl.pallas_call(functools.partial(attend_kernel, scale), out_shape=jax.Sha...  5.6 us
    unnamed x15, local copies, waits for them, and re-layouts  3.42 us
    pallas_call x1, Pallas kernels, body(): pl.pallas_call(combine_kernel, out_shape=jax.ShapeDtypeStruct((tok, size)...  1.91 us
  transfers between devices with their start and end apart: 7, of which 4 were waited for; matrix products, arithmetic and copies ran while one was open for 2% of the time, Pallas kernels for 0%

profile of v2, /device:TPU:6, one launch (start us, length us, event | category | flops | bytes accessed | tf_op | source)
XLA Modules:
  0.0 87.5 jit_solution(15279084104998601484)
XLA Ops:
  0.0 2.5 %copy.27 = bf16[1,128,16,256]{3,1,2,0:T(8,128)(2,1)} copy(bf16[1,128,16,256]{3,2,1,0:T(8,128)(2,1)} %param.6) | data formatting | bytes 2097152 | tf_op args[1]
  2.6 13.4 %all-to-all-start = ((bf16[16,128,256]{2,1,0:T(8,128)(2,1)}), bf16[16,128,256]{2,1,0:T(8,128)(2,1)S(1)}, u32[]{:S(2)}, u32[]{:S(2)}) async-start(bf16[16,128,256]{2,1,0:T(8,128)(2,1)} %bitcast.24), calls=%async_computation | async-start | bytes 2097152 | tf_op jit(solution)/shard_map/all_to_all | solution.py:208
  16.0 7.7 %collective-permute-start = (bf16[1,128,128]{2,1,0:T(8,128)(2,1)S(1)}, bf16[1,128,128]{2,1,0:T(8,128)(2,1)S(1)}, u32[]{:S(2)}, u32[]{:S(2)}) collective-permute-start(bf16[1,128,128]{2,1,0:T(8,128)(2,1)S(1)} %slice_bitcast_fusion), channel_id=1, source_target_pairs={{0,8},{1,9},{2,10},{3,11},{4,12},{5,13},{6,14},{7,15},{8,0},{9,1},... | collective-permute-start | bytes 98312 | tf_op jit(solution)/shard_map/ppermute | solution.py:205
  23.7 1.9 %collective-permute-start.5 = (bf16[128,256]{1,0:T(8,128)(2,1)S(1)}, bf16[128,256]{1,0:T(8,128)(2,1)S(1)}, u32[]{:S(2)}, u32[]{:S(2)}) collective-permute-start(bf16[128,256]{1,0:T(8,128)(2,1)S(1)} %slice.9.now_own), channel_id=1, source_target_pairs={{0,1},{1,0},{2,3},{3,2},{4,5},{5,4},{6,7},{7,6},{8,9},{9,8},{10,11... | collective-permute-start | bytes 196616 | tf_op jit(solution)/shard_map/ppermute | solution.py:205
  25.7 4.6 %collective-permute-start.1 = (bf16[2,128,128]{2,1,0:T(8,128)(2,1)S(1)}, bf16[2,128,128]{2,1,0:T(8,128)(2,1)S(1)}, u32[]{:S(2)}, u32[]{:S(2)}) collective-permute-start(bf16[2,128,128]{2,1,0:T(8,128)(2,1)S(1)} %pad_maximum_fusion.2), channel_id=1, source_target_pairs={{0,4},{1,5},{2,6},{3,7},{4,0},{5,1},{6,2},{7,3},{8,12},{9,13},{10,... | collective-permute-start | bytes 196616 | tf_op jit(solution)/shard_map/ppermute | solution.py:205
  30.3 0.1 constant_dynamic-slice_fusion.1
  30.6 3.8 %collective-permute-done.1 = bf16[2,128,128]{2,1,0:T(8,128)(2,1)S(1)} collective-permute-done((bf16[2,128,128]{2,1,0:T(8,128)(2,1)S(1)}, bf16[2,128,128]{2,1,0:T(8,128)(2,1)S(1)}, u32[]{:S(2)}, u32[]{:S(2)}) %collective-permute-start.1) | collective-permute-done | bytes 65568 | tf_op jit(solution)/shard_map/ppermute | solution.py:205
  34.5 2.0 %collective-permute-start.2 = (bf16[4,128,128]{2,1,0:T(8,128)(2,1)S(1)}, bf16[4,128,128]{2,1,0:T(8,128)(2,1)S(1)}, u32[]{:S(2)}, u32[]{:S(2)}) collective-permute-start(bf16[4,128,128]{2,1,0:T(8,128)(2,1)S(1)} %pad_maximum_fusion.1), channel_id=1, source_target_pairs={{0,2},{1,3},{2,0},{3,1},{4,6},{5,7},{6,4},{7,5},{8,10},{9,11},{10,... | collective-permute-start | bytes 393224 | tf_op jit(solution)/shard_map/ppermute | solution.py:205
  36.5 5.2 %collective-permute-done.2 = bf16[4,128,128]{2,1,0:T(8,128)(2,1)S(1)} collective-permute-done((bf16[4,128,128]{2,1,0:T(8,128)(2,1)S(1)}, bf16[4,128,128]{2,1,0:T(8,128)(2,1)S(1)}, u32[]{:S(2)}, u32[]{:S(2)}) %collective-permute-start.2) | collective-permute-done | bytes 131104 | tf_op jit(solution)/shard_map/ppermute | solution.py:205
  41.7 3.4 %collective-permute-start.3 = (bf16[8,128,128]{2,1,0:T(8,128)(2,1)S(1)}, bf16[8,128,128]{2,1,0:T(8,128)(2,1)S(1)}, u32[]{:S(2)}, u32[]{:S(2)}) collective-permute-start(bf16[8,128,128]{2,1,0:T(8,128)(2,1)S(1)} %pad_maximum_fusion), channel_id=1, source_target_pairs={{0,16},{1,17},{2,18},{3,19},{4,20},{5,21},{6,22},{7,23},{8,24},{9,... | collective-permute-start | bytes 786440 | tf_op jit(solution)/shard_map/ppermute | solution.py:205
  45.1 5.7 %collective-permute-done.3 = bf16[8,128,128]{2,1,0:T(8,128)(2,1)S(1)} collective-permute-done((bf16[8,128,128]{2,1,0:T(8,128)(2,1)S(1)}, bf16[8,128,128]{2,1,0:T(8,128)(2,1)S(1)}, u32[]{:S(2)}, u32[]{:S(2)}) %collective-permute-start.3) | collective-permute-done | bytes 262176 | tf_op jit(solution)/shard_map/ppermute | solution.py:205
  50.9 1.9 %collective-permute-start.4 = (bf16[16,128,256]{2,1,0:T(8,128)(2,1)S(1)}, bf16[16,128,256]{2,1,0:T(8,128)(2,1)S(1)}, u32[]{:S(2)}, u32[]{:S(2)}) collective-permute-start(bf16[16,128,256]{2,1,0:T(8,128)(2,1)S(1)} %all-to-all-done.past_own), channel_id=1, source_target_pairs={{0,1},{1,0},{2,3},{3,2},{4,5},{5,4},{6,7},{7,6},{8,9},{9,8},{10,11... | collective-permute-start | bytes 3145736 | tf_op jit(solution)/shard_map/ppermute | solution.py:205
  52.9 0.1 copy.20
  53.0 0.1 copy.21
  53.1 0.2 maximum_reduce_fusion
  53.3 0.2 convert_reduce_fusion
  53.5 0.1 select_reduce_fusion.3
  53.8 0.1 reshape.100
  53.9 0.6 copy-done.3
  54.5 0.2 select_reduce_fusion.4
  54.8 0.7 collective-permute-done.4.past_other
  55.4 5.6 %attend.1 = bf16[16,144,128]{2,1,0:T(8,128)(2,1)S(1)} custom-call(s32[80]{0:T(128)S(1)} %pad_add_fusion.1.table, bf16[16,128,128]{2,1,0:T(8,128)(2,1)S(1)} %constant_dynamic-update-slice_fusion.q_ref, bf16[16,128,256]{2,1,0:T(8,128)(2,1)S(1)} %all-to-all-done.past_own, bf16[128,256]{1,0:T(8,128)(2,1)S(1)} %slice.9.now_own, ...), custom_call_target="tpu_custom_call" | custom-call | tf_op jit(solution)/shard_map/attend/pallas_call | solution.py:122
  61.0 24.5 %all_to_all.10.in_ref = bf16[16,144,128]{2,1,0:T(8,128)(2,1)} all-to-all(bf16[16,144,128]{2,1,0:T(8,128)(2,1)S(1)} %attend.1), channel_id=1, replica_groups={{0,2,4,6,8,10,12,14,16,18,20,22,24,26,28,30},{1,3,5,7,9,11,13,15,17,19,..., dimensions={0} | all-to-all | bytes 1179648 | tf_op jit(solution)/shard_map/all_to_all | solution.py:222
  85.6 1.9 %combine.1 = bf16[128,128]{1,0:T(8,128)(2,1)} custom-call(bf16[16,144,128]{2,1,0:T(8,128)(2,1)} %all_to_all.10.in_ref), custom_call_target="tpu_custom_call" | custom-call | tf_op jit(solution)/shard_map/combine/pallas_call | solution.py:225
  (30 shorter events, 0.6 us)
Async XLA Ops:
  2.6 13.4 %copy-start = (bf16[128,1,384]{2,0,1:T(8,128)(2,1)S(1)}, bf16[128,1,384]{2,0,1:T(8,128)(2,1)}, u32[]{:S(2)}) copy-start(bf16[128,1,384]{2,0,1:T(8,128)(2,1)} %param.5) | copy-start | bytes 294916
  2.6 48.3 %all-to-all-start = ((bf16[16,128,256]{2,1,0:T(8,128)(2,1)}), bf16[16,128,256]{2,1,0:T(8,128)(2,1)S(1)}, u32[]{:S(2)}, u32[]{:S(2)}) async-start(bf16[16,128,256]{2,1,0:T(8,128)(2,1)} %bitcast.24), calls=%async_computation | async-start | bytes 2097152 | tf_op jit(solution)/shard_map/all_to_all | solution.py:208
  16.0 9.8 %collective-permute-start = (bf16[1,128,128]{2,1,0:T(8,128)(2,1)S(1)}, bf16[1,128,128]{2,1,0:T(8,128)(2,1)S(1)}, u32[]{:S(2)}, u32[]{:S(2)}) collective-permute-start(bf16[1,128,128]{2,1,0:T(8,128)(2,1)S(1)} %slice_bitcast_fusion), channel_id=1, source_target_pairs={{0,8},{1,9},{2,10},{3,11},{4,12},{5,13},{6,14},{7,15},{8,0},{9,1},... | collective-permute-start | bytes 98312 | tf_op jit(solution)/shard_map/ppermute | solution.py:205
  23.7 31.1 %collective-permute-start.5 = (bf16[128,256]{1,0:T(8,128)(2,1)S(1)}, bf16[128,256]{1,0:T(8,128)(2,1)S(1)}, u32[]{:S(2)}, u32[]{:S(2)}) collective-permute-start(bf16[128,256]{1,0:T(8,128)(2,1)S(1)} %slice.9.now_own), channel_id=1, source_target_pairs={{0,1},{1,0},{2,3},{3,2},{4,5},{5,4},{6,7},{7,6},{8,9},{9,8},{10,11... | collective-permute-start | bytes 196616 | tf_op jit(solution)/shard_map/ppermute | solution.py:205
  25.7 4.6 %copy-start.1 = (s32[32,32]{1,0:T(8,128)S(1)}, s32[32,32]{1,0:T(8,128)}, u32[]{:S(2)}) copy-start(s32[32,32]{1,0:T(8,128)} %param.9) | copy-start | bytes 12292
  25.7 8.7 %collective-permute-start.1 = (bf16[2,128,128]{2,1,0:T(8,128)(2,1)S(1)}, bf16[2,128,128]{2,1,0:T(8,128)(2,1)S(1)}, u32[]{:S(2)}, u32[]{:S(2)}) collective-permute-start(bf16[2,128,128]{2,1,0:T(8,128)(2,1)S(1)} %pad_maximum_fusion.2), channel_id=1, source_target_pairs={{0,4},{1,5},{2,6},{3,7},{4,0},{5,1},{6,2},{7,3},{8,12},{9,13},{10,... | collective-permute-start | bytes 196616 | tf_op jit(solution)/shard_map/ppermute | solution.py:205
  34.5 7.2 %collective-permute-start.2 = (bf16[4,128,128]{2,1,0:T(8,128)(2,1)S(1)}, bf16[4,128,128]{2,1,0:T(8,128)(2,1)S(1)}, u32[]{:S(2)}, u32[]{:S(2)}) collective-permute-start(bf16[4,128,128]{2,1,0:T(8,128)(2,1)S(1)} %pad_maximum_fusion.1), channel_id=1, source_target_pairs={{0,2},{1,3},{2,0},{3,1},{4,6},{5,7},{6,4},{7,5},{8,10},{9,11},{10,... | collective-permute-start | bytes 393224 | tf_op jit(solution)/shard_map/ppermute | solution.py:205
  41.7 9.1 %collective-permute-start.3 = (bf16[8,128,128]{2,1,0:T(8,128)(2,1)S(1)}, bf16[8,128,128]{2,1,0:T(8,128)(2,1)S(1)}, u32[]{:S(2)}, u32[]{:S(2)}) collective-permute-start(bf16[8,128,128]{2,1,0:T(8,128)(2,1)S(1)} %pad_maximum_fusion), channel_id=1, source_target_pairs={{0,16},{1,17},{2,18},{3,19},{4,20},{5,21},{6,22},{7,23},{8,24},{9,... | collective-permute-start | bytes 786440 | tf_op jit(solution)/shard_map/ppermute | solution.py:205
  50.9 2.0 %copy-start.2 = (s32[32]{0:T(128)S(1)}, s32[32]{0:T(128)}, u32[]{:S(2)}) copy-start(s32[32]{0:T(128)} %param.8) | copy-start | bytes 388
  50.9 4.6 %collective-permute-start.4 = (bf16[16,128,256]{2,1,0:T(8,128)(2,1)S(1)}, bf16[16,128,256]{2,1,0:T(8,128)(2,1)S(1)}, u32[]{:S(2)}, u32[]{:S(2)}) collective-permute-start(bf16[16,128,256]{2,1,0:T(8,128)(2,1)S(1)} %all-to-all-done.past_own), channel_id=1, source_target_pairs={{0,1},{1,0},{2,3},{3,2},{4,5},{5,4},{6,7},{7,6},{8,9},{9,8},{10,11... | collective-permute-start | bytes 3145736 | tf_op jit(solution)/shard_map/ppermute | solution.py:205
  53.9 0.7 copy-start.3

commit v3 on v2

v3 whole, which is shorter than its diff:
```python
import functools
import math

import jax
import jax.numpy as jnp
from jax import lax
from jax.experimental import pallas as pl
from jax.experimental.pallas import tpu as pltpu
from jax.sharding import PartitionSpec as P

NEG = -1e30
LSE_ROWS = 16
GROUP = 4


def slot_buckets(slots):
    sizes = [size for size in (1, 2, 3, 4, 5, 6, 7, 8, 9, 11, 13, 15) if size < slots]
    return sizes + [slots]


def attend_kernel(scale, merge, *refs):
    if merge:
        table, queries, past, now, near_part, far_part, out_ref, values, scores = refs
    else:
        table, queries, past, now, out_ref, values, scores = refs
    tiles, tok, size = queries.shape
    slots = past.shape[0] + 1
    members = min(GROUP, tiles)

    def block_of(slot):
        return now[...] if slot == 0 else past[table[slot - 1]]

    for slot in range(slots):
        values[:size, slot * tok : (slot + 1) * tok] = block_of(slot)[:, size:].T
    values[size:, :] = jnp.ones((LSE_ROWS, slots * tok), jnp.bfloat16)
    row_ids = lax.broadcasted_iota(jnp.int32, (LSE_ROWS, tok), 0)
    if merge:
        half = tiles // 2
        start = table[slots - 1]
        out_ref[pl.ds(start, half)] = near_part[...]
        out_ref[pl.ds(half - start, half)] = far_part[...]

    def one_group(group, _):
        base = slots + group * (3 * members)
        group_tiles = [table[base + member * 3] for member in range(members)]
        places = [table[base + member * 3 + 1] for member in range(members)]
        limits = [table[base + member * 3 + 2] for member in range(members)]
        most = functools.reduce(jnp.maximum, limits)

        if not merge:

            @pl.when(most == 0)
            def _():
                for tile in group_tiles:
                    out_ref[tile, :size, :] = jnp.zeros((size, tok), jnp.bfloat16)
                    out_ref[tile, size:, :] = jnp.where(row_ids == 0, NEG, 0.0).astype(jnp.bfloat16)

        def work(count):
            lanes = jnp.concatenate([queries[place].T for place in places], 1)
            peaks = [jnp.full((8, tok), NEG, jnp.float32) for _ in range(members)]
            for slot in range(count):
                raw = jnp.dot(block_of(slot)[:, :size], lanes, preferred_element_type=jnp.float32)
                scores[slot * tok : (slot + 1) * tok, :] = raw
                for member in range(members):
                    best = jnp.max(
                        raw[:, member * tok : (member + 1) * tok].reshape(tok // 8, 8, tok), axis=0
                    )
                    best = jnp.where(slot < limits[member], best, NEG)
                    peaks[member] = jnp.maximum(peaks[member], best)
            peaks = [jnp.max(peak, axis=0, keepdims=True) for peak in peaks]
            summed = None
            for low_slot in range(0, count, 2):
                chunk = []
                for slot in range(low_slot, min(low_slot + 2, count)):
                    shift = jnp.concatenate(
                        [jnp.where(slot < limits[member], peaks[member], -NEG) for member in range(members)], 1
                    )
                    chunk.append(
                        jnp.exp2(
                            (scores[slot * tok : (slot + 1) * tok, :] - shift) * (scale * math.log2(math.e))
                        ).astype(jnp.bfloat16)
                    )
                term = jnp.dot(
                    values[:, low_slot * tok : (low_slot + len(chunk)) * tok],
                    jnp.concatenate(chunk, 0),
                    preferred_element_type=jnp.float32,
                )
                summed = term if summed is None else summed + term
            total = jnp.maximum(summed[size : size + 1, :], 1.0)
            share = summed[:size, :] / total
            lse = jnp.concatenate(peaks, 1) * scale + jnp.log(total)
            if merge:
                others = [out_ref[tile] for tile in group_tiles]
                other_lse = jnp.concatenate(
                    [jnp.sum(other[size:, :].astype(jnp.float32), axis=0, keepdims=True) for other in others], 1
                )
                other_share = jnp.concatenate([other[:size, :] for other in others], 1).astype(jnp.float32)
                top = jnp.maximum(lse, other_lse)
                mine, theirs = jnp.exp(lse - top), jnp.exp(other_lse - top)
                both = mine + theirs
                share = share * (mine / both) + other_share * (theirs / both)
                lse = top + jnp.log(both)
            share = share.astype(jnp.bfloat16)
            high = lse.astype(jnp.bfloat16).astype(jnp.float32)
            rest = lse - high
            middle = rest.astype(jnp.bfloat16).astype(jnp.float32)
            low_part = rest - middle
            for member, tile in enumerate(group_tiles):
                cut = slice(member * tok, (member + 1) * tok)
                rows = jnp.where(row_ids == 0, high[:, cut], 0.0)
                rows = jnp.where(row_ids == 1, middle[:, cut], rows)
                rows = jnp.where(row_ids == 2, low_part[:, cut], rows)
                out_ref[tile, :size, :] = share[:, cut]
                out_ref[tile, size:, :] = rows.astype(jnp.bfloat16)

        low = 0
        for count in slot_buckets(slots):
            pl.when((most > low) & (most <= count))(functools.partial(work, count))
            low = count
        return 0

    lax.fori_loop(0, tiles // members, one_group, 0)


def attend_call(scale, table, queries, past, now, parts=()):
    tiles, tok, size = queries.shape
    slots = past.shape[0] + 1
    vmem = pl.BlockSpec(memory_space=pltpu.VMEM)
    return pl.pallas_call(
        functools.partial(attend_kernel, scale, bool(parts)),
        out_shape=jax.ShapeDtypeStruct((tiles, size + LSE_ROWS, tok), jnp.bfloat16),
        in_specs=[pl.BlockSpec(memory_space=pltpu.SMEM)] + [vmem] * (3 + len(parts)),
        out_specs=vmem,
        scratch_shapes=[
            pltpu.VMEM((size + LSE_ROWS, slots * tok), jnp.bfloat16),
            pltpu.VMEM((slots * tok, min(GROUP, tiles) * tok), jnp.float32),
        ],
        compiler_params=pltpu.CompilerParams(vmem_limit_bytes=32 * 2**20),
        cost_estimate=pl.CostEstimate(
            flops=10**6 * tiles, bytes_accessed=10**5, transcendentals=10**3 * tiles
        ),
        name="attend_last" if parts else "attend",
    )(table, queries, past, now, *parts)


def combine_kernel(in_ref, out_ref):
    tiles = in_ref.shape[0]
    tok, size = out_ref.shape
    lse = jnp.concatenate(
        [
            jnp.sum(in_ref[tile, size:, :].astype(jnp.float32), axis=0, keepdims=True)
            for tile in range(tiles)
        ],
        0,
    )
    factor = jnp.exp(lse - jnp.max(lse, axis=0, keepdims=True))
    factor = factor / jnp.sum(factor, axis=0, keepdims=True)
    total = in_ref[0, :size, :].astype(jnp.float32) * factor[0:1]
    for tile in range(1, tiles):
        total += in_ref[tile, :size, :].astype(jnp.float32) * factor[tile : tile + 1]
    out_ref[...] = total.T.astype(jnp.bfloat16)


def gather_bits(tiles):
    bits = [1 << k for k in range(tiles.bit_length() - 1)]
    return bits[-2::-1] + bits[-1:]


def ordered_table(by_rank, start, tile_ids, places, slots):
    count = slots.shape[0]
    ids = jnp.arange(count, dtype=jnp.int32)
    before = (slots[None, :] > slots[:, None]) | ((slots[None, :] == slots[:, None]) & (ids[None, :] < ids[:, None]))
    rank = jnp.sum(before.astype(jnp.int32), axis=1)
    chosen = rank[None, :] == ids[:, None]
    columns = jnp.stack([tile_ids, places, slots], 1)
    ordered = jnp.sum(jnp.where(chosen[:, :, None], columns[None], 0), axis=1)
    return jnp.concatenate([by_rank, start.reshape(1), ordered.reshape(-1)]).astype(jnp.int32)


def work_tables(frame_rank, frame_depth, tile_lists, position, core, tiles, frames):
    half_tiles = tiles // 2
    ids = jnp.arange(frames, dtype=jnp.int32)
    by_rank = jnp.sum(jnp.where(frame_rank[None, :] == (frames - 1 - ids)[:, None], ids[None, :], 0), axis=1)
    own = 2 * position + core
    mine = lax.dynamic_index_in_dim(tile_lists.reshape(tiles, 2, 2 * tiles), core, 1, False)
    depth = lax.dynamic_index_in_dim(frame_depth.reshape(tiles, 2), core, 1, False) + 1

    def slots_of(key_tile):
        return jnp.where(lax.dynamic_index_in_dim(mine, key_tile, 1, False) == 1, depth, 0)

    own_slots, other_slots = slots_of(own), slots_of(own + 1 - 2 * core)
    tile_ids = jnp.arange(tiles, dtype=jnp.int32)
    apart = tile_ids ^ position
    places = jnp.zeros_like(tile_ids)
    for k, bit in enumerate(gather_bits(tiles)):
        places = places + jnp.where((apart & bit) != 0, 1 << k, 0)
    start = position // half_tiles * half_tiles
    tables = []
    for first in (start, half_tiles - start):
        part_slots = lax.dynamic_slice_in_dim(own_slots, first, half_tiles)
        part_places = lax.dynamic_slice_in_dim(places, first, half_tiles) % half_tiles
        tables.append(ordered_table(by_rank, start, tile_ids[:half_tiles], part_places, part_slots))
    return tables + [ordered_table(by_rank, start, tile_ids, places, other_slots)]


def body(qkv_now, past_cache, frame_rank, frame_depth, tile_lists):
    tok = qkv_now.shape[0]
    size = qkv_now.shape[2] // 3
    space = lax.axis_size("space")
    frames = lax.axis_size("frame")
    tiles = space // 2
    index = lax.axis_index("space")
    position, core = index // 2, index % 2
    scale = 1.0 / math.sqrt(size)

    def swap(array, bit):
        return lax.ppermute(array, "space", [(i, i ^ bit) for i in range(space)])

    by_head = past_cache[0].transpose(1, 0, 2)
    by_head, qkv_now = lax.optimization_barrier((by_head, qkv_now))
    past_own = lax.all_to_all(by_head, "frame", split_axis=0, concat_axis=0, tiled=True)

    now = qkv_now[:, 0, :]
    near = now[None, :, :size]
    *bits, last_bit = gather_bits(tiles)
    for step, bit in enumerate(bits):
        near = jnp.concatenate([near, swap(near, 2 * bit)], 0)
        if step == 1:
            near, frame_rank, frame_depth, tile_lists = lax.optimization_barrier(
                (near, frame_rank, frame_depth, tile_lists)
            )
    now_own = now[:, size:]
    now_other = swap(now_own, 1)
    tables = work_tables(frame_rank, frame_depth, tile_lists, position, core, tiles, frames)

    far = swap(near, 2 * last_bit)
    near_part = attend_call(scale, tables[0], near, past_own, now_own)
    past_own, far, near_part, now_other = lax.optimization_barrier((past_own, far, near_part, now_other))
    past_other = swap(past_own, 1)
    far_part = attend_call(scale, tables[1], far, past_own, now_own)
    queries = jnp.concatenate([near, far], 0)
    partial = attend_call(scale, tables[2], queries, past_other, now_other, (near_part, far_part))
    groups = [[2 * place + which for place in range(tiles)] for which in range(2)]
    received = lax.all_to_all(
        partial, "space", split_axis=0, concat_axis=0, axis_index_groups=groups, tiled=True
    )
    return pl.pallas_call(
        combine_kernel,
        out_shape=jax.ShapeDtypeStruct((tok, size), jnp.bfloat16),
        compiler_params=pltpu.CompilerParams(vmem_limit_bytes=8 * 2**20),
        name="combine",
    )(received)


def solution(mesh):
    in_specs = (P("space", "frame", None), P("frame", "space", None, None), P(), P(), P())
    out_specs = P("space", "frame")
    return jax.shard_map(body, mesh=mesh, in_specs=in_specs, out_specs=out_specs, check_vma=False)
```

time: 88.1 us -> 88.3 us (level)
  waiting for transfers between devices: 15.3 us -> 10.4 us
  Pallas kernels: 7.51 us -> 9.31 us
  blocking collectives: 24.5 us -> 25.9 us
  other arithmetic: 0.88 us -> 1.81 us
  local copies, waits for them, and re-layouts: 4.01 us -> 4.92 us
    ppermute x6, waiting for transfers between devices: 15.3 us -> 10.4 us  [swap(): return lax.ppermute(array, 'space', [(i, i ^ bit) for i in range(space)])]
    pallas_call x1 -> x3, Pallas kernels: 5.6 us -> 8.46 us  [attend_call(): pl.pallas_call(functools.partial(attend_kernel, scale, bool(parts)), out_...]
    all_to_all x1, blocking collectives: 24.5 us -> 25.9 us  [body(): lax.all_to_all(partial, 'space', split_axis=0, concat_axis=0, axis_index_...]
    pallas_call x1, Pallas kernels: 1.91 us -> 0.85 us  [body(): pl.pallas_call(combine_kernel, out_shape=jax.ShapeDtypeStruct((tok, size)...]
    unnamed x15 -> x12, local copies, waits for them, and re-layouts: 3.42 us -> 3.93 us
  transfers between devices with their start and end apart: 7 -> 7, of which waited for: 4 -> 3; matrix products, arithmetic and copies ran while one was open for 2% -> 3% of each run, Pallas kernels for 0% -> 6%
where the time goes in v3:
time: 88.3 us; the launch traced here: 87.7 us
  starting transfers between devices  35 us (40%)
  blocking collectives  25.9 us (29%)
  waiting for transfers between devices  10.4 us (12%)
  Pallas kernels  9.31 us (11%)
  local copies, waits for them, and re-layouts  4.92 us (6%)
  other arithmetic  1.81 us (2%)
    all_to_all x1, blocking collectives, body(): lax.all_to_all(partial, 'space', split_axis=0, concat_axis=0, axis_index_...  25.9 us
    ppermute x6, starting transfers between devices, swap(): return lax.ppermute(array, 'space', [(i, i ^ bit) for i in range(space)])  21.7 us
    all_to_all x1, starting transfers between devices, body(): lax.all_to_all(by_head, 'frame', split_axis=0, concat_axis=0, tiled=True)  13.4 us
    ppermute x6, waiting for transfers between devices, swap(): return lax.ppermute(array, 'space', [(i, i ^ bit) for i in range(space)])  10.4 us
    pallas_call x3, Pallas kernels, attend_call(): pl.pallas_call(functools.partial(attend_kernel, scale, bool(parts)), out_...  8.46 us
    unnamed x12, local copies, waits for them, and re-layouts  3.93 us
  transfers between devices with their start and end apart: 7, of which 3 were waited for; matrix products, arithmetic and copies ran while one was open for 3% of the time, Pallas kernels for 6%

profile of v3, /device:TPU:6, one launch (start us, length us, event | category | flops | bytes accessed | tf_op | source)
XLA Modules:
  0.0 87.7 jit_solution(11795572043070725200)
XLA Ops:
  0.0 2.5 %copy.38 = bf16[1,128,16,256]{3,1,2,0:T(8,128)(2,1)} copy(bf16[1,128,16,256]{3,2,1,0:T(8,128)(2,1)} %param.6) | data formatting | bytes 2097152 | tf_op args[1]
  2.6 13.4 %all-to-all-start = ((bf16[16,128,256]{2,1,0:T(8,128)(2,1)}), bf16[16,128,256]{2,1,0:T(8,128)(2,1)S(1)}, u32[]{:S(2)}, u32[]{:S(2)}) async-start(bf16[16,128,256]{2,1,0:T(8,128)(2,1)} %bitcast.23), calls=%async_computation | async-start | bytes 2097152 | tf_op jit(solution)/shard_map/all_to_all | solution.py:221
  16.0 7.7 %collective-permute-start = (bf16[1,128,128]{2,1,0:T(8,128)(2,1)S(1)}, bf16[1,128,128]{2,1,0:T(8,128)(2,1)S(1)}, u32[]{:S(2)}, u32[]{:S(2)}) collective-permute-start(bf16[1,128,128]{2,1,0:T(8,128)(2,1)S(1)} %slice_bitcast_fusion), channel_id=1, source_target_pairs={{0,8},{1,9},{2,10},{3,11},{4,12},{5,13},{6,14},{7,15},{8,0},{9,1},... | collective-permute-start | bytes 98312 | tf_op jit(solution)/shard_map/ppermute | solution.py:217
  23.7 1.9 %collective-permute-start.4 = (bf16[128,256]{1,0:T(8,128)(2,1)S(1)}, bf16[128,256]{1,0:T(8,128)(2,1)S(1)}, u32[]{:S(2)}, u32[]{:S(2)}) collective-permute-start(bf16[128,256]{1,0:T(8,128)(2,1)S(1)} %slice.16.refs_3_), channel_id=1, source_target_pairs={{0,1},{1,0},{2,3},{3,2},{4,5},{5,4},{6,7},{7,6},{8,9},{9,8},{10,11... | collective-permute-start | bytes 196616 | tf_op jit(solution)/shard_map/ppermute | solution.py:217
  25.8 4.6 %collective-permute-start.1 = (bf16[2,128,128]{2,1,0:T(8,128)(2,1)S(1)}, bf16[2,128,128]{2,1,0:T(8,128)(2,1)S(1)}, u32[]{:S(2)}, u32[]{:S(2)}) collective-permute-start(bf16[2,128,128]{2,1,0:T(8,128)(2,1)S(1)} %pad_maximum_fusion.2), channel_id=1, source_target_pairs={{0,4},{1,5},{2,6},{3,7},{4,0},{5,1},{6,2},{7,3},{8,12},{9,13},{10,... | collective-permute-start | bytes 196616 | tf_op jit(solution)/shard_map/ppermute | solution.py:217
  30.4 4.1 %collective-permute-done.1 = bf16[2,128,128]{2,1,0:T(8,128)(2,1)S(1)} collective-permute-done((bf16[2,128,128]{2,1,0:T(8,128)(2,1)S(1)}, bf16[2,128,128]{2,1,0:T(8,128)(2,1)S(1)}, u32[]{:S(2)}, u32[]{:S(2)}) %collective-permute-start.1) | collective-permute-done | bytes 65568 | tf_op jit(solution)/shard_map/ppermute | solution.py:217
  34.6 0.6 copy-done.1
  35.6 2.0 %collective-permute-start.2 = (bf16[4,128,128]{2,1,0:T(8,128)(2,1)S(1)}, bf16[4,128,128]{2,1,0:T(8,128)(2,1)S(1)}, u32[]{:S(2)}, u32[]{:S(2)}) collective-permute-start(bf16[4,128,128]{2,1,0:T(8,128)(2,1)S(1)} %pad_maximum_fusion.1), channel_id=1, source_target_pairs={{0,2},{1,3},{2,0},{3,1},{4,6},{5,7},{6,4},{7,5},{8,10},{9,11},{10,... | collective-permute-start | bytes 393224 | tf_op jit(solution)/shard_map/ppermute | solution.py:217
  37.5 0.2 fusion.17
  37.9 0.2 convert_reduce_fusion.1
  38.1 0.2 convert_reduce_fusion.2
  38.5 4.3 %collective-permute-done.2 = bf16[4,128,128]{2,1,0:T(8,128)(2,1)S(1)} collective-permute-done((bf16[4,128,128]{2,1,0:T(8,128)(2,1)S(1)}, bf16[4,128,128]{2,1,0:T(8,128)(2,1)S(1)}, u32[]{:S(2)}, u32[]{:S(2)}) %collective-permute-start.2) | collective-permute-done | bytes 131104 | tf_op jit(solution)/shard_map/ppermute | solution.py:217
  42.8 3.4 %collective-permute-start.3 = (bf16[8,128,128]{2,1,0:T(8,128)(2,1)S(1)}, bf16[8,128,128]{2,1,0:T(8,128)(2,1)S(1)}, u32[]{:S(2)}, u32[]{:S(2)}) collective-permute-start(bf16[8,128,128]{2,1,0:T(8,128)(2,1)S(1)} %constant_dynamic-update-slice_fusion.refs_1_), channel_id=1, source_target_pairs={{0,16},{1,17},{2,18},{3,19},{4,20},{5,21},{6,22},{7,23},{8,24},{9,... | collective-permute-start | bytes 786440 | tf_op jit(solution)/shard_map/ppermute | solution.py:217
  46.6 0.6 copy-done.3
  47.2 0.2 select_reduce_fusion.3
  47.5 2.4 %attend.2.refs_4_ = bf16[8,144,128]{2,1,0:T(8,128)(2,1)S(1)} custom-call(s32[41]{0:T(128)S(1)} %get-tuple-element.31.refs_0_, bf16[8,128,128]{2,1,0:T(8,128)(2,1)S(1)} %constant_dynamic-update-slice_fusion.refs_1_, bf16[16,128,256]{2,1,0:T(8,128)(2,1)S(1)} %all-to-all-done.refs_2_, bf16[128,256]{1,0:T(8,128)(2,1)S(1)} %slice.16.refs_3_), custom_call_target="tpu_custom_call" | custom-call | flops 8000000 | bytes 100000 | tf_op jit(solution)/shard_map/attend/pallas_call | solution.py:129
  49.9 2.0 %collective-permute-done.3.refs_1_ = bf16[8,128,128]{2,1,0:T(8,128)(2,1)S(1)} collective-permute-done((bf16[8,128,128]{2,1,0:T(8,128)(2,1)S(1)}, bf16[8,128,128]{2,1,0:T(8,128)(2,1)S(1)}, u32[]{:S(2)}, u32[]{:S(2)}) %collective-permute-start.3) | collective-permute-done | bytes 262176 | tf_op jit(solution)/shard_map/ppermute | solution.py:217
  51.9 2.1 %collective-permute-start.5 = (bf16[16,128,256]{2,1,0:T(8,128)(2,1)S(1)}, bf16[16,128,256]{2,1,0:T(8,128)(2,1)S(1)}, u32[]{:S(2)}, u32[]{:S(2)}) collective-permute-start(bf16[16,128,256]{2,1,0:T(8,128)(2,1)S(1)} %all-to-all-done.refs_2_), channel_id=1, source_target_pairs={{0,1},{1,0},{2,3},{3,2},{4,5},{5,4},{6,7},{7,6},{8,9},{9,8},{10,11... | collective-permute-start | bytes 3145736 | tf_op jit(solution)/shard_map/ppermute | solution.py:217
  54.2 0.2 convert_reduce_fusion
  54.4 0.1 select_reduce_fusion
  54.8 2.5 %attend.3.refs_5_ = bf16[8,144,128]{2,1,0:T(8,128)(2,1)S(1)} custom-call(s32[41]{0:T(128)S(1)} %get-tuple-element.30.refs_0_, bf16[8,128,128]{2,1,0:T(8,128)(2,1)S(1)} %collective-permute-done.3.refs_1_, bf16[16,128,256]{2,1,0:T(8,128)(2,1)S(1)} %all-to-all-done.refs_2_, bf16[128,256]{1,0:T(8,128)(2,1)S(1)} %slice.16.refs_3_), custom_call_target="tpu_custom_call" | custom-call | flops 8000000 | bytes 100000 | tf_op jit(solution)/shard_map/attend/pallas_call | solution.py:129
  57.4 3.6 %attend_last.1 = bf16[16,144,128]{2,1,0:T(8,128)(2,1)S(1)} custom-call(s32[65]{0:T(128)S(1)} %pad_add_fusion.3.refs_0_, bf16[16,128,128]{2,1,0:T(8,128)(2,1)S(1)} %pad_maximum_fusion.refs_1_, bf16[16,128,256]{2,1,0:T(8,128)(2,1)S(1)} %collective-permute-done.5.refs_2_, bf16[128,256]{1,0:T(8,128)(2,1)S(1)} %collective-permute-done.4.refs_3_, ...), custom_call_target="tpu_custom_call" | custom-call | flops 16000000 | bytes 100000 | tf_op jit(solution)/shard_map/attend_last/pallas_call | solution.py:129
  61.0 25.9 %all_to_all.10.in_ref = bf16[16,144,128]{2,1,0:T(8,128)(2,1)S(1)} all-to-all(bf16[16,144,128]{2,1,0:T(8,128)(2,1)S(1)} %attend_last.1), channel_id=1, replica_groups={{0,2,4,6,8,10,12,14,16,18,20,22,24,26,28,30},{1,3,5,7,9,11,13,15,17,19,..., dimensions={0} | all-to-all | bytes 1179648 | tf_op jit(solution)/shard_map/all_to_all | solution.py:244
  86.9 0.8 combine.1
  (47 shorter events, 1.9 us)
Async XLA Ops:
  2.6 13.4 %copy-start = (bf16[128,1,384]{2,0,1:T(8,128)(2,1)S(1)}, bf16[128,1,384]{2,0,1:T(8,128)(2,1)}, u32[]{:S(2)}) copy-start(bf16[128,1,384]{2,0,1:T(8,128)(2,1)} %param.5) | copy-start | bytes 294916
  2.6 44.9 %all-to-all-start = ((bf16[16,128,256]{2,1,0:T(8,128)(2,1)}), bf16[16,128,256]{2,1,0:T(8,128)(2,1)S(1)}, u32[]{:S(2)}, u32[]{:S(2)}) async-start(bf16[16,128,256]{2,1,0:T(8,128)(2,1)} %bitcast.23), calls=%async_computation | async-start | bytes 2097152 | tf_op jit(solution)/shard_map/all_to_all | solution.py:221
  16.0 9.8 %collective-permute-start = (bf16[1,128,128]{2,1,0:T(8,128)(2,1)S(1)}, bf16[1,128,128]{2,1,0:T(8,128)(2,1)S(1)}, u32[]{:S(2)}, u32[]{:S(2)}) collective-permute-start(bf16[1,128,128]{2,1,0:T(8,128)(2,1)S(1)} %slice_bitcast_fusion), channel_id=1, source_target_pairs={{0,8},{1,9},{2,10},{3,11},{4,12},{5,13},{6,14},{7,15},{8,0},{9,1},... | collective-permute-start | bytes 98312 | tf_op jit(solution)/shard_map/ppermute | solution.py:217
  23.7 26.1 %collective-permute-start.4 = (bf16[128,256]{1,0:T(8,128)(2,1)S(1)}, bf16[128,256]{1,0:T(8,128)(2,1)S(1)}, u32[]{:S(2)}, u32[]{:S(2)}) collective-permute-start(bf16[128,256]{1,0:T(8,128)(2,1)S(1)} %slice.16.refs_3_), channel_id=1, source_target_pairs={{0,1},{1,0},{2,3},{3,2},{4,5},{5,4},{6,7},{7,6},{8,9},{9,8},{10,11... | collective-permute-start | bytes 196616 | tf_op jit(solution)/shard_map/ppermute | solution.py:217
  25.8 8.7 %collective-permute-start.1 = (bf16[2,128,128]{2,1,0:T(8,128)(2,1)S(1)}, bf16[2,128,128]{2,1,0:T(8,128)(2,1)S(1)}, u32[]{:S(2)}, u32[]{:S(2)}) collective-permute-start(bf16[2,128,128]{2,1,0:T(8,128)(2,1)S(1)} %pad_maximum_fusion.2), channel_id=1, source_target_pairs={{0,4},{1,5},{2,6},{3,7},{4,0},{5,1},{6,2},{7,3},{8,12},{9,13},{10,... | collective-permute-start | bytes 196616 | tf_op jit(solution)/shard_map/ppermute | solution.py:217
  30.3 4.1 %copy-start.2 = (s32[32]{0:T(128)S(1)}, s32[32]{0:T(128)}, u32[]{:S(2)}) copy-start(s32[32]{0:T(128)} %param.8) | copy-start | bytes 388
  34.5 0.7 copy-start.1
  35.6 7.2 %collective-permute-start.2 = (bf16[4,128,128]{2,1,0:T(8,128)(2,1)S(1)}, bf16[4,128,128]{2,1,0:T(8,128)(2,1)S(1)}, u32[]{:S(2)}, u32[]{:S(2)}) collective-permute-start(bf16[4,128,128]{2,1,0:T(8,128)(2,1)S(1)} %pad_maximum_fusion.1), channel_id=1, source_target_pairs={{0,2},{1,3},{2,0},{3,1},{4,6},{5,7},{6,4},{7,5},{8,10},{9,11},{10,... | collective-permute-start | bytes 393224 | tf_op jit(solution)/shard_map/ppermute | solution.py:217
  42.8 9.1 %collective-permute-start.3 = (bf16[8,128,128]{2,1,0:T(8,128)(2,1)S(1)}, bf16[8,128,128]{2,1,0:T(8,128)(2,1)S(1)}, u32[]{:S(2)}, u32[]{:S(2)}) collective-permute-start(bf16[8,128,128]{2,1,0:T(8,128)(2,1)S(1)} %constant_dynamic-update-slice_fusion.refs_1_), channel_id=1, source_target_pairs={{0,16},{1,17},{2,18},{3,19},{4,20},{5,21},{6,22},{7,23},{8,24},{9,... | collective-permute-start | bytes 786440 | tf_op jit(solution)/shard_map/ppermute | solution.py:217
  46.6 0.7 copy-start.3
  51.9 5.5 %collective-permute-start.5 = (bf16[16,128,256]{2,1,0:T(8,128)(2,1)S(1)}, bf16[16,128,256]{2,1,0:T(8,128)(2,1)S(1)}, u32[]{:S(2)}, u32[]{:S(2)}) collective-permute-start(bf16[16,128,256]{2,1,0:T(8,128)(2,1)S(1)} %all-to-all-done.refs_2_), channel_id=1, source_target_pairs={{0,1},{1,0},{2,3},{3,2},{4,5},{5,4},{6,7},{7,6},{8,9},{9,8},{10,11... | collective-permute-start | bytes 3145736 | tf_op jit(solution)/shard_map/ppermute | solution.py:217

commit v4 on v3

--- a/solution.py
+++ b/solution.py
@@ -177,8 +177,7 @@
     return jnp.concatenate([by_rank, start.reshape(1), ordered.reshape(-1)]).astype(jnp.int32)
 
 
-def work_tables(frame_rank, frame_depth, tile_lists, position, core, tiles, frames):
-    half_tiles = tiles // 2
+def visible_slots(frame_rank, frame_depth, tile_lists, position, core, tiles, frames):
     ids = jnp.arange(frames, dtype=jnp.int32)
     by_rank = jnp.sum(jnp.where(frame_rank[None, :] == (frames - 1 - ids)[:, None], ids[None, :], 0), axis=1)
     own = 2 * position + core
@@ -188,7 +187,12 @@
     def slots_of(key_tile):
         return jnp.where(lax.dynamic_index_in_dim(mine, key_tile, 1, False) == 1, depth, 0)
 
-    own_slots, other_slots = slots_of(own), slots_of(own + 1 - 2 * core)
+    return by_rank, slots_of(own), slots_of(own + 1 - 2 * core)
+
+
+def work_tables(by_rank, own_slots, other_slots, position):
+    tiles = own_slots.shape[0]
+    half_tiles = tiles // 2
     tile_ids = jnp.arange(tiles, dtype=jnp.int32)
     apart = tile_ids ^ position
     places = jnp.zeros_like(tile_ids)
@@ -222,16 +226,15 @@
 
     now = qkv_now[:, 0, :]
     near = now[None, :, :size]
+    slots = visible_slots(frame_rank, frame_depth, tile_lists, position, core, tiles, frames)
     *bits, last_bit = gather_bits(tiles)
     for step, bit in enumerate(bits):
         near = jnp.concatenate([near, swap(near, 2 * bit)], 0)
         if step == 1:
-            near, frame_rank, frame_depth, tile_lists = lax.optimization_barrier(
-                (near, frame_rank, frame_depth, tile_lists)
-            )
+            near, slots = lax.optimization_barrier((near, slots))
     now_own = now[:, size:]
     now_other = swap(now_own, 1)
-    tables = work_tables(frame_rank, frame_depth, tile_lists, position, core, tiles, frames)
+    tables = work_tables(*slots, position)
 
     far = swap(near, 2 * last_bit)
     near_part = attend_call(scale, tables[0], near, past_own, now_own)

time: 88.3 us -> 87.9 us (level)
  Pallas kernels: 9.31 us -> 11.1 us
  waiting for transfers between devices: 10.4 us -> 12.1 us
  blocking collectives: 25.9 us -> 24.3 us
  starting transfers between devices: 35 us -> 33.7 us
    pallas_call x3, Pallas kernels: 8.46 us -> 10.3 us  [attend_call(): pl.pallas_call(functools.partial(attend_kernel, scale, bool(parts)), out_...]
    ppermute x6, waiting for transfers between devices: 10.4 us -> 12.1 us  [swap(): return lax.ppermute(array, 'space', [(i, i ^ bit) for i in range(space)])]
    all_to_all x1, blocking collectives: 25.9 us -> 24.3 us  [body(): lax.all_to_all(partial, 'space', split_axis=0, concat_axis=0, axis_index_...]
    ppermute x6, starting transfers between devices: 21.7 us -> 20.3 us  [swap(): return lax.ppermute(array, 'space', [(i, i ^ bit) for i in range(space)])]
where the time goes in v4:
time: 87.9 us; the launch traced here: 87.5 us
  starting transfers between devices  33.7 us (38%)
  blocking collectives  24.3 us (28%)
  waiting for transfers between devices  12.1 us (14%)
  Pallas kernels  11.1 us (13%)
  local copies, waits for them, and re-layouts  4.28 us (5%)
  other arithmetic  1.68 us (2%)
    all_to_all x1, blocking collectives, body(): lax.all_to_all(partial, 'space', split_axis=0, concat_axis=0, axis_index_...  24.3 us
    ppermute x6, starting transfers between devices, swap(): return lax.ppermute(array, 'space', [(i, i ^ bit) for i in range(space)])  20.3 us
    all_to_all x1, starting transfers between devices, body(): lax.all_to_all(by_head, 'frame', split_axis=0, concat_axis=0, tiled=True)  13.4 us
    ppermute x6, waiting for transfers between devices, swap(): return lax.ppermute(array, 'space', [(i, i ^ bit) for i in range(space)])  12.1 us
    pallas_call x3, Pallas kernels, attend_call(): pl.pallas_call(functools.partial(attend_kernel, scale, bool(parts)), out_...  10.3 us
    unnamed x12, local copies, waits for them, and re-layouts  3.31 us
  transfers between devices with their start and end apart: 7, of which 3 were waited for; matrix products, arithmetic and copies ran while one was open for 3% of the time, Pallas kernels for 6%

profile of v4, /device:TPU:6, one launch (start us, length us, event | category | flops | bytes accessed | tf_op | source)
XLA Modules:
  0.0 87.5 jit_solution(4649714221863635221)
XLA Ops:
  0.0 2.5 %copy.36 = bf16[1,128,16,256]{3,1,2,0:T(8,128)(2,1)} copy(bf16[1,128,16,256]{3,2,1,0:T(8,128)(2,1)} %param.6) | data formatting | bytes 2097152 | tf_op args[1]
  2.6 13.4 %all-to-all-start = ((bf16[16,128,256]{2,1,0:T(8,128)(2,1)}), bf16[16,128,256]{2,1,0:T(8,128)(2,1)S(1)}, u32[]{:S(2)}, u32[]{:S(2)}) async-start(bf16[16,128,256]{2,1,0:T(8,128)(2,1)} %bitcast.22), calls=%async_computation | async-start | bytes 2097152 | tf_op jit(solution)/shard_map/all_to_all | solution.py:225
  16.0 7.7 %collective-permute-start = (bf16[1,128,128]{2,1,0:T(8,128)(2,1)S(1)}, bf16[1,128,128]{2,1,0:T(8,128)(2,1)S(1)}, u32[]{:S(2)}, u32[]{:S(2)}) collective-permute-start(bf16[1,128,128]{2,1,0:T(8,128)(2,1)S(1)} %slice_bitcast_fusion), channel_id=1, source_target_pairs={{0,8},{1,9},{2,10},{3,11},{4,12},{5,13},{6,14},{7,15},{8,0},{9,1},... | collective-permute-start | bytes 98312 | tf_op jit(solution)/shard_map/ppermute | solution.py:221
  23.7 1.9 %collective-permute-start.4 = (bf16[128,256]{1,0:T(8,128)(2,1)S(1)}, bf16[128,256]{1,0:T(8,128)(2,1)S(1)}, u32[]{:S(2)}, u32[]{:S(2)}) collective-permute-start(bf16[128,256]{1,0:T(8,128)(2,1)S(1)} %slice.16.refs_3_), channel_id=1, source_target_pairs={{0,1},{1,0},{2,3},{3,2},{4,5},{5,4},{6,7},{7,6},{8,9},{9,8},{10,11... | collective-permute-start | bytes 196616 | tf_op jit(solution)/shard_map/ppermute | solution.py:221
  25.8 0.6 copy-done.2
  26.4 0.2 add_reduce_fusion
  27.0 3.3 %collective-permute-start.1 = (bf16[2,128,128]{2,1,0:T(8,128)(2,1)S(1)}, bf16[2,128,128]{2,1,0:T(8,128)(2,1)S(1)}, u32[]{:S(2)}, u32[]{:S(2)}) collective-permute-start(bf16[2,128,128]{2,1,0:T(8,128)(2,1)S(1)} %pad_maximum_fusion.2), channel_id=1, source_target_pairs={{0,4},{1,5},{2,6},{3,7},{4,0},{5,1},{6,2},{7,3},{8,12},{9,13},{10,... | collective-permute-start | bytes 196616 | tf_op jit(solution)/shard_map/ppermute | solution.py:221
  30.3 0.2 select_reduce_fusion.3
  30.5 5.2 %collective-permute-done.1 = bf16[2,128,128]{2,1,0:T(8,128)(2,1)S(1)} collective-permute-done((bf16[2,128,128]{2,1,0:T(8,128)(2,1)S(1)}, bf16[2,128,128]{2,1,0:T(8,128)(2,1)S(1)}, u32[]{:S(2)}, u32[]{:S(2)}) %collective-permute-start.1) | collective-permute-done | bytes 65568 | tf_op jit(solution)/shard_map/ppermute | solution.py:221
  35.7 1.9 %collective-permute-start.2 = (bf16[4,128,128]{2,1,0:T(8,128)(2,1)S(1)}, bf16[4,128,128]{2,1,0:T(8,128)(2,1)S(1)}, u32[]{:S(2)}, u32[]{:S(2)}) collective-permute-start(bf16[4,128,128]{2,1,0:T(8,128)(2,1)S(1)} %pad_maximum_fusion.1), channel_id=1, source_target_pairs={{0,2},{1,3},{2,0},{3,1},{4,6},{5,7},{6,4},{7,5},{8,10},{9,11},{10,... | collective-permute-start | bytes 393224 | tf_op jit(solution)/shard_map/ppermute | solution.py:221
  37.8 0.2 convert_reduce_fusion.1
  38.0 4.9 %collective-permute-done.2 = bf16[4,128,128]{2,1,0:T(8,128)(2,1)S(1)} collective-permute-done((bf16[4,128,128]{2,1,0:T(8,128)(2,1)S(1)}, bf16[4,128,128]{2,1,0:T(8,128)(2,1)S(1)}, u32[]{:S(2)}, u32[]{:S(2)}) %collective-permute-start.2) | collective-permute-done | bytes 131104 | tf_op jit(solution)/shard_map/ppermute | solution.py:221
  43.0 3.4 %collective-permute-start.3 = (bf16[8,128,128]{2,1,0:T(8,128)(2,1)S(1)}, bf16[8,128,128]{2,1,0:T(8,128)(2,1)S(1)}, u32[]{:S(2)}, u32[]{:S(2)}) collective-permute-start(bf16[8,128,128]{2,1,0:T(8,128)(2,1)S(1)} %constant_dynamic-update-slice_fusion.refs_1_), channel_id=1, source_target_pairs={{0,16},{1,17},{2,18},{3,19},{4,20},{5,21},{6,22},{7,23},{8,24},{9,... | collective-permute-start | bytes 786440 | tf_op jit(solution)/shard_map/ppermute | solution.py:221
  46.4 0.1 select_reduce_fusion.2
  46.7 0.2 select_reduce_fusion.1
  47.1 3.0 %attend.2.refs_4_ = bf16[8,144,128]{2,1,0:T(8,128)(2,1)S(1)} custom-call(s32[41]{0:T(128)S(1)} %get-tuple-element.28.refs_0_, bf16[8,128,128]{2,1,0:T(8,128)(2,1)S(1)} %constant_dynamic-update-slice_fusion.refs_1_, bf16[16,128,256]{2,1,0:T(8,128)(2,1)S(1)} %all-to-all-done.refs_2_, bf16[128,256]{1,0:T(8,128)(2,1)S(1)} %slice.16.refs_3_), custom_call_target="tpu_custom_call" | custom-call | flops 8000000 | bytes 100000 | tf_op jit(solution)/shard_map/attend/pallas_call | solution.py:129
  50.1 2.0 %collective-permute-done.3.refs_1_ = bf16[8,128,128]{2,1,0:T(8,128)(2,1)S(1)} collective-permute-done((bf16[8,128,128]{2,1,0:T(8,128)(2,1)S(1)}, bf16[8,128,128]{2,1,0:T(8,128)(2,1)S(1)}, u32[]{:S(2)}, u32[]{:S(2)}) %collective-permute-start.3) | collective-permute-done | bytes 262176 | tf_op jit(solution)/shard_map/ppermute | solution.py:221
  52.1 2.1 %collective-permute-start.5 = (bf16[16,128,256]{2,1,0:T(8,128)(2,1)S(1)}, bf16[16,128,256]{2,1,0:T(8,128)(2,1)S(1)}, u32[]{:S(2)}, u32[]{:S(2)}) collective-permute-start(bf16[16,128,256]{2,1,0:T(8,128)(2,1)S(1)} %all-to-all-done.refs_2_), channel_id=1, source_target_pairs={{0,1},{1,0},{2,3},{3,2},{4,5},{5,4},{6,7},{7,6},{8,9},{9,8},{10,11... | collective-permute-start | bytes 3145736 | tf_op jit(solution)/shard_map/ppermute | solution.py:221
  54.5 0.2 convert_reduce_fusion
  54.7 0.1 select_reduce_fusion
  55.1 2.5 %attend.3.refs_5_ = bf16[8,144,128]{2,1,0:T(8,128)(2,1)S(1)} custom-call(s32[41]{0:T(128)S(1)} %get-tuple-element.27.refs_0_, bf16[8,128,128]{2,1,0:T(8,128)(2,1)S(1)} %collective-permute-done.3.refs_1_, bf16[16,128,256]{2,1,0:T(8,128)(2,1)S(1)} %all-to-all-done.refs_2_, bf16[128,256]{1,0:T(8,128)(2,1)S(1)} %slice.16.refs_3_), custom_call_target="tpu_custom_call" | custom-call | flops 8000000 | bytes 100000 | tf_op jit(solution)/shard_map/attend/pallas_call | solution.py:129
  57.7 4.7 %attend_last.1 = bf16[16,144,128]{2,1,0:T(8,128)(2,1)S(1)} custom-call(s32[65]{0:T(128)S(1)} %pad_add_fusion.3.refs_0_, bf16[16,128,128]{2,1,0:T(8,128)(2,1)S(1)} %pad_maximum_fusion.refs_1_, bf16[16,128,256]{2,1,0:T(8,128)(2,1)S(1)} %collective-permute-done.5.refs_2_, bf16[128,256]{1,0:T(8,128)(2,1)S(1)} %collective-permute-done.4.refs_3_, ...), custom_call_target="tpu_custom_call" | custom-call | flops 16000000 | bytes 100000 | tf_op jit(solution)/shard_map/attend_last/pallas_call | solution.py:129
  62.4 24.3 %all_to_all.10.in_ref = bf16[16,144,128]{2,1,0:T(8,128)(2,1)S(1)} all-to-all(bf16[16,144,128]{2,1,0:T(8,128)(2,1)S(1)} %attend_last.1), channel_id=1, replica_groups={{0,2,4,6,8,10,12,14,16,18,20,22,24,26,28,30},{1,3,5,7,9,11,13,15,17,19,..., dimensions={0} | all-to-all | bytes 1179648 | tf_op jit(solution)/shard_map/all_to_all | solution.py:247
  86.7 0.8 combine.1
  (45 shorter events, 1.6 us)
Async XLA Ops:
  2.6 13.4 %copy-start = (bf16[128,1,384]{2,0,1:T(8,128)(2,1)S(1)}, bf16[128,1,384]{2,0,1:T(8,128)(2,1)}, u32[]{:S(2)}) copy-start(bf16[128,1,384]{2,0,1:T(8,128)(2,1)} %param.5) | copy-start | bytes 294916
  2.6 44.5 %all-to-all-start = ((bf16[16,128,256]{2,1,0:T(8,128)(2,1)}), bf16[16,128,256]{2,1,0:T(8,128)(2,1)S(1)}, u32[]{:S(2)}, u32[]{:S(2)}) async-start(bf16[16,128,256]{2,1,0:T(8,128)(2,1)} %bitcast.22), calls=%async_computation | async-start | bytes 2097152 | tf_op jit(solution)/shard_map/all_to_all | solution.py:225
  16.0 11.1 %collective-permute-start = (bf16[1,128,128]{2,1,0:T(8,128)(2,1)S(1)}, bf16[1,128,128]{2,1,0:T(8,128)(2,1)S(1)}, u32[]{:S(2)}, u32[]{:S(2)}) collective-permute-start(bf16[1,128,128]{2,1,0:T(8,128)(2,1)S(1)} %slice_bitcast_fusion), channel_id=1, source_target_pairs={{0,8},{1,9},{2,10},{3,11},{4,12},{5,13},{6,14},{7,15},{8,0},{9,1},... | collective-permute-start | bytes 98312 | tf_op jit(solution)/shard_map/ppermute | solution.py:221
  23.7 26.4 %collective-permute-start.4 = (bf16[128,256]{1,0:T(8,128)(2,1)S(1)}, bf16[128,256]{1,0:T(8,128)(2,1)S(1)}, u32[]{:S(2)}, u32[]{:S(2)}) collective-permute-start(bf16[128,256]{1,0:T(8,128)(2,1)S(1)} %slice.16.refs_3_), channel_id=1, source_target_pairs={{0,1},{1,0},{2,3},{3,2},{4,5},{5,4},{6,7},{7,6},{8,9},{9,8},{10,11... | collective-permute-start | bytes 196616 | tf_op jit(solution)/shard_map/ppermute | solution.py:221
  25.7 0.7 copy-start.2
  25.7 0.9 %copy-start.1 = (s32[32,32]{1,0:T(8,128)S(1)}, s32[32,32]{1,0:T(8,128)}, u32[]{:S(2)}) copy-start(s32[32,32]{1,0:T(8,128)} %param.9) | copy-start | bytes 12292
  27.0 3.3 %copy-start.3 = (s32[16]{0:T(128)S(1)}, s32[16]{0:T(128)}, u32[]{:S(2)}) copy-start(s32[16]{0:T(128)} %param.7) | copy-start | bytes 196
  27.0 8.7 %collective-permute-start.1 = (bf16[2,128,128]{2,1,0:T(8,128)(2,1)S(1)}, bf16[2,128,128]{2,1,0:T(8,128)(2,1)S(1)}, u32[]{:S(2)}, u32[]{:S(2)}) collective-permute-start(bf16[2,128,128]{2,1,0:T(8,128)(2,1)S(1)} %pad_maximum_fusion.2), channel_id=1, source_target_pairs={{0,4},{1,5},{2,6},{3,7},{4,0},{5,1},{6,2},{7,3},{8,12},{9,13},{10,... | collective-permute-start | bytes 196616 | tf_op jit(solution)/shard_map/ppermute | solution.py:221
  35.7 7.2 %collective-permute-start.2 = (bf16[4,128,128]{2,1,0:T(8,128)(2,1)S(1)}, bf16[4,128,128]{2,1,0:T(8,128)(2,1)S(1)}, u32[]{:S(2)}, u32[]{:S(2)}) collective-permute-start(bf16[4,128,128]{2,1,0:T(8,128)(2,1)S(1)} %pad_maximum_fusion.1), channel_id=1, source_target_pairs={{0,2},{1,3},{2,0},{3,1},{4,6},{5,7},{6,4},{7,5},{8,10},{9,11},{10,... | collective-permute-start | bytes 393224 | tf_op jit(solution)/shard_map/ppermute | solution.py:221
  43.0 9.1 %collective-permute-start.3 = (bf16[8,128,128]{2,1,0:T(8,128)(2,1)S(1)}, bf16[8,128,128]{2,1,0:T(8,128)(2,1)S(1)}, u32[]{:S(2)}, u32[]{:S(2)}) collective-permute-start(bf16[8,128,128]{2,1,0:T(8,128)(2,1)S(1)} %constant_dynamic-update-slice_fusion.refs_1_), channel_id=1, source_target_pairs={{0,16},{1,17},{2,18},{3,19},{4,20},{5,21},{6,22},{7,23},{8,24},{9,... | collective-permute-start | bytes 786440 | tf_op jit(solution)/shard_map/ppermute | solution.py:221
  52.1 5.6 %collective-permute-start.5 = (bf16[16,128,256]{2,1,0:T(8,128)(2,1)S(1)}, bf16[16,128,256]{2,1,0:T(8,128)(2,1)S(1)}, u32[]{:S(2)}, u32[]{:S(2)}) collective-permute-start(bf16[16,128,256]{2,1,0:T(8,128)(2,1)S(1)} %all-to-all-done.refs_2_), channel_id=1, source_target_pairs={{0,1},{1,0},{2,3},{3,2},{4,5},{5,4},{6,7},{7,6},{8,9},{9,8},{10,11... | collective-permute-start | bytes 3145736 | tf_op jit(solution)/shard_map/ppermute | solution.py:221
